TPU v7x, 128 devices: a whole 4x4x4 slice. The times are simulated.
128 devices in a mesh: ctx: 16 (over x, y), head: 8 (over z, core).
Axes of the slice: x: 4, y: 4, z: 4, core: 2. Of those that a mesh axis runs over, the one named last changes fastest.
Arguments:
- tokens: bfloat16 [65536, 2048], P(('ctx', 'head')), may hold values from -6 to 6
- picks: int32 [16384], P(('ctx', 'head')), may hold values from 0 to 511, as said below
- counts: int32 [128], P(('ctx', 'head')), may hold values from 1 to 128, 8192 in all
- score: float32 [16384], P(('ctx', 'head')), may hold values from 0.25 to 1
- w_in: bfloat16 [2048, 8192], P(None, 'head'), may hold values from -0.125 to 0.125
- w_out: bfloat16 [8192, 2048], P('head'), may hold values from -0.0625 to 0.0625
- cotan: bfloat16 [16384, 2048], P(('ctx', 'head')), may hold values from -6 to 6
Outputs:
- heavy: bfloat16 [16384, 2048], P(('ctx', 'head'))
- grad_x: bfloat16 [65536, 2048], P(('ctx', 'head'))
- grad_score: float32 [16384], P(('ctx', 'head'))
- grad_in: float32 [2048, 8192], P('ctx', 'head')
- grad_out: float32 [8192, 2048], P('head', 'ctx')
Inputs may be any that keep to these rules, and one draw needn't show every extreme that they name: `picks`: the 128 entries of one device are distinct positions of that device's 512 tokens.
All inputs are finite; a program needn't handle non-finite values. No bound on the sum of `counts` on one device may be relied on, other than what follows from the above.
Results may differ from a plain program's by a relative error of at most 0.027.
Values may be sent and summed in bfloat16 or wider, within the bound.
No kernel may reach another device: no remote copies, remote signals or barrier semaphores. Data moves between devices by JAX's collectives and lax.ppermute only.
A program may use at most 128 MiB of HBM per device.

v0:
```python
import functools

import jax
import jax.numpy as jnp
from jax import lax
from jax.experimental import pallas as pl
from jax.experimental.pallas import tpu as pltpu
from jax.sharding import PartitionSpec as P

F32 = jnp.float32
BF16 = jnp.bfloat16
SIDE = 4
MIB = 1024 * 1024
LITTLE = pl.CostEstimate(flops=1, bytes_accessed=1, transcendentals=0)


def gelu_parts(u):
    c = 0.7978845608
    t = jnp.tanh(c * (u + 0.044715 * u * u * u))
    value = 0.5 * u * (1.0 + t)
    slope = 0.5 * (1.0 + t) + 0.5 * u * (1.0 - t * t) * c * (1.0 + 3.0 * 0.044715 * u * u)
    return (value, slope)


def move_x(v, by):
    perm = [(x * SIDE + y, ((x + by) % SIDE) * SIDE + y) for x in range(SIDE) for y in range(SIDE)]
    return lax.ppermute(v, "ctx", perm)


def move_y(v, by):
    perm = [(x * SIDE + y, x * SIDE + (y + by) % SIDE) for x in range(SIDE) for y in range(SIDE)]
    return lax.ppermute(v, "ctx", perm)


def move_lane(v, by):
    perm = [(z * 2 + c, ((z + (by if c == 0 else -by)) % SIDE) * 2 + c) for z in range(SIDE) for c in range(2)]
    return lax.ppermute(v, "head", perm)


def swap_core(v):
    return lax.ppermute(v, "head", [(i, i ^ 1) for i in range(2 * SIDE)])


def dot(a, b, dims):
    return lax.dot_general(a, b, ((dims[0], dims[1]), ((), ())), preferred_element_type=F32)


def params(mib):
    return pltpu.CompilerParams(vmem_limit_bytes=mib * MIB)


def whole(a):
    return pl.BlockSpec(a.shape, lambda *_: (0,) * a.ndim)


def take_rows(tokens, picks, counts, score, cotan):
    routed = picks.shape[0]
    n_tok, width = tokens.shape

    def body(counts_ref, tokens_ref, picks_ref, score_ref, cotan_ref, out_ref, me_ref):
        me_ref[0] = lax.axis_index("ctx").astype(jnp.int32)
        me_ref[1] = lax.axis_index("head").astype(jnp.int32)
        places = lax.broadcasted_iota(jnp.int32, (n_tok, routed), 0)
        slots = lax.broadcasted_iota(jnp.int32, (n_tok, routed), 1)
        hit = (places == picks_ref[...]) & (slots < counts_ref[0])
        one_hot = jnp.where(hit, 1.0, 0.0).astype(BF16)
        out_ref[0] = dot(one_hot, tokens_ref[...], ((0,), (0,))).astype(BF16)
        across = lax.broadcasted_iota(jnp.int32, (routed, routed), 0)
        along = lax.broadcasted_iota(jnp.int32, (routed, routed), 1)
        kept = (across == along) & (along < counts_ref[0])
        factor = jnp.sum(jnp.where(kept, score_ref[...], 0.0), axis=1, keepdims=True)
        out_ref[1] = (factor * cotan_ref[...].astype(F32)).astype(BF16)

    return pl.pallas_call(
        body,
        grid_spec=pltpu.PrefetchScalarGridSpec(
            num_scalar_prefetch=1,
            grid=(1,),
            in_specs=[
                whole(tokens),
                pl.BlockSpec((1, routed), lambda i, c: (0, 0)),
                pl.BlockSpec((1, routed), lambda i, c: (0, 0)),
                whole(cotan),
            ],
            out_specs=[
                pl.BlockSpec((2, routed, width), lambda i, c: (0, 0, 0)),
                pl.BlockSpec(memory_space=pltpu.SMEM),
            ],
        ),
        out_shape=[jax.ShapeDtypeStruct((2, routed, width), BF16), jax.ShapeDtypeStruct((2,), jnp.int32)],
        compiler_params=params(60),
        cost_estimate=LITTLE,
        name="take_rows",
    )(counts, tokens, picks[None, :], score[None, :], cotan)


def hidden_units(packs, w_in, w_out):
    n = len(packs)
    _, piece, width = packs[0].shape
    count = n * piece
    hid = w_in.shape[1]
    tile = hid // SIDE
    quarter = width // SIDE
    strip = quarter // SIDE

    def body(*refs):
        r = jnp.concatenate([ref[0] for ref in refs[:n]], axis=0)
        d = jnp.concatenate([ref[1] for ref in refs[:n]], axis=0)
        win_ref, wout_ref, hidden_ref, dpre_ref, turned_ref = refs[n:]
        pre = dot(r, win_ref[...], ((1,), (0,)))
        dhid = dot(d, wout_ref[...], ((1,), (1,)))
        value, slope = gelu_parts(pre)
        hidden_ref[...] = value.astype(BF16)
        dpre_ref[...] = (dhid * slope).astype(BF16)
        y = pl.program_id(0)
        for x in range(SIDE):
            at = pl.multiple_of(x * quarter + y * strip, strip)
            for k in range(n):
                turned_ref[pl.ds(k * piece, piece), pl.ds(x * strip, strip)] = refs[k][1, :, pl.ds(at, strip)]

    return pl.pallas_call(
        body,
        grid=(SIDE,),
        in_specs=[whole(a) for a in packs]
        + [
            pl.BlockSpec((width, tile), lambda j: (0, j)),
            pl.BlockSpec((tile, width), lambda j: (j, 0)),
        ],
        out_specs=[
            pl.BlockSpec((count, tile), lambda j: (0, j)),
            pl.BlockSpec((count, tile), lambda j: (0, j)),
            pl.BlockSpec((count, quarter), lambda j: (0, j)),
        ],
        out_shape=[
            jax.ShapeDtypeStruct((count, hid), BF16),
            jax.ShapeDtypeStruct((count, hid), BF16),
            jax.ShapeDtypeStruct((count, width), BF16),
        ],
        compiler_params=params(4 + count // 64),
        cost_estimate=LITTLE,
        name="hidden_units",
    )(*packs, held(w_in), held(w_out))


def hold(w_in, w_out):
    def body(win_ref, wout_ref, win_out, wout_out, sems):
        copies = [
            pltpu.make_async_copy(win_ref, win_out, sems.at[0]),
            pltpu.make_async_copy(wout_ref, wout_out, sems.at[1]),
        ]
        for copy in copies:
            copy.start()
        for copy in copies:
            copy.wait()

    return pl.pallas_call(
        body,
        in_specs=[pl.BlockSpec(memory_space=pl.ANY)] * 2,
        out_specs=[pl.BlockSpec(memory_space=pltpu.VMEM)] * 2,
        out_shape=[pltpu.VMEM(w.shape, w.dtype) for w in (w_in, w_out)],
        scratch_shapes=[pltpu.SemaphoreType.DMA((2,))],
        compiler_params=params(4),
        cost_estimate=LITTLE,
        name="hold_weights",
    )(pltpu.with_memory_space_constraint(w_in, pltpu.HBM), pltpu.with_memory_space_constraint(w_out, pltpu.HBM))


def held(w):
    return pltpu.with_memory_space_constraint(w, pltpu.VMEM)


def in_hbm(arrays):
    return [pltpu.with_memory_space_constraint(a, pltpu.HBM) for a in arrays]


def owners(head):
    chip, core = head // 2, lax.rem(head, 2)
    back = 1 + 2 * core
    here, behind = chip, lax.rem(chip + SIDE - back, SIDE)
    ahead, far = lax.rem(chip + back, SIDE), lax.rem(chip + 2, SIDE)
    rest = 1 - core
    return [
        here * 2 + core, here * 2 + rest,
        behind * 2 + core, ahead * 2 + rest,
        behind * 2 + rest, ahead * 2 + core,
        far * 2 + core, far * 2 + rest,
    ]


def row_terms(hidden, dpre, w_in, w_out, piece):
    count, hid = hidden.shape
    width = w_in.shape[0]
    n = count // piece
    tile = width // SIDE

    def body(hidden_ref, dpre_ref, win_ref, wout_ref, out_ref):
        ffn = dot(hidden_ref[...], wout_ref[...], ((1,), (0,))).astype(BF16)
        dx = dot(dpre_ref[...], win_ref[...], ((1,), (1,))).astype(BF16)
        for s, v in enumerate((ffn, dx)):
            for k in range(n):
                out_ref[k, s] = v[k * piece : (k + 1) * piece]

    return pl.pallas_call(
        body,
        grid=(SIDE,),
        in_specs=[
            whole(hidden),
            whole(dpre),
            pl.BlockSpec((tile, hid), lambda j: (j, 0)),
            pl.BlockSpec((hid, tile), lambda j: (0, j)),
        ],
        out_specs=pl.BlockSpec((n, 2, piece, tile), lambda j: (0, 0, 0, j)),
        out_shape=jax.ShapeDtypeStruct((n, 2, piece, width), BF16),
        compiler_params=params(8),
        cost_estimate=LITTLE,
        name="row_terms",
    )(hidden, dpre, held(w_in), held(w_out))


def all_terms(me, earlier, hidden, dpre, w_in, w_out, piece):
    count, hid = hidden.shape
    width = w_in.shape[0]
    n = count // piece
    tile = width // SIDE
    total = n + sum(a.shape[0] for a in earlier)

    def body(me_ref, *refs):
        hidden_ref, dpre_ref, win_ref, wout_ref, out_ref = refs[len(earlier) :]
        to = owners(me_ref[1])
        at = 0
        for ref in refs[: len(earlier)]:
            for k in range(ref.shape[0]):
                out_ref[to[at]] = ref[k]
                at += 1
        ffn = dot(hidden_ref[...], wout_ref[...], ((1,), (0,))).astype(BF16)
        dx = dot(dpre_ref[...], win_ref[...], ((1,), (1,))).astype(BF16)
        for k in range(n):
            for s, v in enumerate((ffn, dx)):
                out_ref[to[at + k], s] = v[k * piece : (k + 1) * piece]

    def terms(a):
        return pl.BlockSpec((a.shape[0], 2, piece, tile), lambda j, h: (0, 0, 0, j))

    return pl.pallas_call(
        body,
        grid_spec=pltpu.PrefetchScalarGridSpec(
            num_scalar_prefetch=1,
            grid=(SIDE,),
            in_specs=[terms(a) for a in earlier]
            + [
                whole(hidden),
                whole(dpre),
                pl.BlockSpec((tile, hid), lambda j, h: (j, 0)),
                pl.BlockSpec((hid, tile), lambda j, h: (0, j)),
            ],
            out_specs=pl.BlockSpec((total, 2, piece, tile), lambda j, h: (0, 0, 0, j)),
        ),
        out_shape=pltpu.HBM((total, 2, piece, width), BF16),
        compiler_params=params(14),
        cost_estimate=LITTLE,
        name="all_terms",
    )(me, *earlier, hidden, dpre, held(w_in), held(w_out))


def first_step(i):
    place = jnp.where(i < 2, 2, jnp.where(i == 2, 1, 3))
    half = jnp.where((i == 1) | (i == 2), 1, 0)
    return place, half


def later_step(i):
    place = jnp.where(i >= 2, 0, jnp.where(i == 0, 1, 3))
    half = jnp.where((i == 1) | (i == 3), 1, 0)
    return place, half


def in_blocks(me, packs, dpre, order, split):
    n = len(packs)
    _, piece, width = packs[0].shape
    hid = dpre[0].shape[1]
    size = width // (2 * SIDE)

    def body(me_ref, *refs):
        i = pl.program_id(0)
        r = jnp.concatenate([ref[0] for ref in refs[:n]], axis=0)
        d = jnp.concatenate([ref[...] for ref in refs[n : n + len(dpre)]], axis=0)
        term = dot(r, d, ((0,), (0,))).astype(BF16)
        outs = refs[n + len(dpre) :]
        if split:
            for s in range(2):

                @pl.when(lax.rem(i, 2) == s)
                def _():
                    outs[s][0] = term

        else:
            outs[0][0] = term

    def columns(i, me_ref):
        place, half = order(i)
        return (0, 0, 2 * lax.rem(me_ref[0] // SIDE + place, SIDE) + half)

    return blocks_call(body, me, [pl.BlockSpec((1, piece, size), columns)] * n + [whole(a) for a in dpre],
                       in_hbm(packs + dpre), (size, hid), split, n * piece)


def out_blocks(me, hidden, turned, order, split):
    count = sum(a.shape[0] for a in hidden)
    hid = hidden[0].shape[1]
    quarter = turned[0].shape[1] // SIDE

    def body(me_ref, *refs):
        i = pl.program_id(0)
        n = len(hidden)
        h = jnp.concatenate([ref[...] for ref in refs[:n]], axis=0)
        d = jnp.concatenate([ref[...] for ref in refs[n : 2 * n]], axis=0)
        term = dot(h, d, ((0,), (0,))).astype(BF16)
        outs = refs[2 * n :]
        if split:
            for s in range(2):

                @pl.when(lax.rem(i, 2) == s)
                def _():
                    outs[s][0] = term

        else:
            outs[0][0] = term

    def units(i, me_ref):
        return (0, order(i)[1])

    def columns(i, me_ref):
        return (0, lax.rem(lax.rem(me_ref[0], SIDE) + order(i)[0], SIDE))

    specs = [pl.BlockSpec((a.shape[0], hid // 2), units) for a in hidden]
    specs += [pl.BlockSpec((a.shape[0], quarter), columns) for a in turned]
    return blocks_call(body, me, specs, in_hbm(hidden + turned), (hid // 2, quarter), split, count)


def blocks_call(body, me, specs, args, block, split, count):
    if split:
        shapes = [jax.ShapeDtypeStruct((2,) + block, BF16)] * 2
        outs = [pl.BlockSpec((1,) + block, lambda i, me_ref: (i // 2, 0, 0))] * 2
    else:
        shapes = [jax.ShapeDtypeStruct((4,) + block, BF16)]
        outs = [pl.BlockSpec((1,) + block, lambda i, me_ref: (i, 0, 0))]
    return pl.pallas_call(
        body,
        grid_spec=pltpu.PrefetchScalarGridSpec(
            num_scalar_prefetch=1, grid=(4,), in_specs=specs, out_specs=outs
        ),
        out_shape=shapes,
        compiler_params=params(8),
        cost_estimate=LITTLE,
        name="weight_blocks",
    )(me, *args)


def ring_total(me, later, below0, above0, below1, above1, rowwise):
    block = later.shape[1:]
    if rowwise:
        cut = (2 * block[0] // SIDE, block[1])
    else:
        cut = (2 * block[0], block[1] // SIDE)

    def body(me_ref, later_ref, b0, a0, b1, a1, keep_ref, next_ref, prev_ref, far_ref, sum_ref):
        half = block[0]
        sum_ref[pl.ds(0, half), :] = later_ref[0].astype(F32) + b0[...].astype(F32) + a0[0].astype(F32)
        sum_ref[pl.ds(half, half), :] = later_ref[1].astype(F32) + b1[0].astype(F32) + a1[...].astype(F32)
        if rowwise:
            at = lax.rem(me_ref[0], SIDE)
        else:
            at = me_ref[0] // SIDE
        for k, ref in ((0, keep_ref), (1, next_ref), (3, prev_ref), (2, far_ref)):
            to = lax.rem(at + k, SIDE)
            if rowwise:
                v = sum_ref[pl.ds(pl.multiple_of(to * cut[0], cut[0]), cut[0]), :]
            else:
                v = sum_ref[:, pl.ds(pl.multiple_of(to * cut[1], cut[1]), cut[1])]
            ref[...] = v.astype(ref.dtype)

    second = pl.BlockSpec((2,) + block, lambda i, me_ref: (1, 0, 0))
    one = pl.BlockSpec(block, lambda i, me_ref: (0, 0))
    tail = pl.BlockSpec((1,) + block, lambda i, me_ref: (1, 0, 0))
    out = pl.BlockSpec(cut, lambda i, me_ref: (0, 0))
    return pl.pallas_call(
        body,
        grid_spec=pltpu.PrefetchScalarGridSpec(
            num_scalar_prefetch=1,
            grid=(1,),
            in_specs=[second, one, tail, tail, one],
            out_specs=[out] * 4,
            scratch_shapes=[pltpu.VMEM((2 * block[0], block[1]), F32)],
        ),
        out_shape=[jax.ShapeDtypeStruct(cut, F32)] + [jax.ShapeDtypeStruct(cut, BF16)] * 3,
        compiler_params=params(8),
        cost_estimate=LITTLE,
        name="ring_total",
    )(me, later, below0, above0, below1, above1)


def after(values, *deps):
    return lax.optimization_barrier((values, deps))[0]


def on_device(tokens, picks, counts, score, w_in, w_out, cotan):
    routed = picks.shape[0]
    n_tok = tokens.shape[0]

    own_mine, me = take_rows(tokens, picks, counts, score, cotan)
    w_in, w_out = hold(*after((w_in, w_out), own_mine))
    near_mine = move_lane(own_mine, 1)
    own_other = swap_core(own_mine)
    own_packs = [own_mine, own_other]
    own = hidden_units(own_packs, w_in, w_out)

    near_other = move_lane(own_other, 1)
    near_mine = after(near_mine, own)
    far_mine = move_lane(near_mine, 1)
    near_packs = [near_mine, swap_core(near_mine)]
    near = hidden_units(near_packs, w_in, w_out)
    own_terms = row_terms(own[0], own[1], w_in, w_out, routed)
    near_terms = row_terms(near[0], near[1], w_in, w_out, routed)

    near_other, far_mine = after((near_other, far_mine), near, own_terms, near_terms)
    last_packs = [near_other, swap_core(near_other), far_mine, swap_core(far_mine)]
    last = hidden_units(last_packs, w_in, w_out)
    terms = all_terms(me, [own_terms, near_terms], last[0], last[1], w_in, w_out, routed)
    width = tokens.shape[1]
    sums = lax.psum_scatter(terms.reshape(-1, width), "head", scatter_dimension=0, tiled=True)

    all_packs = own_packs + near_packs + last_packs
    hidden, dpre, turned = ([u[i] for u in (own, near, last)] for i in range(3))
    all_packs, dpre = after((all_packs, dpre), terms)
    in_up, in_down = in_blocks(me, all_packs, dpre, first_step, True)
    in_below, in_above = move_x(in_up, 1), move_x(in_down, -1)
    hidden, turned = after((hidden, turned), in_up, in_down)
    out_up, out_down = out_blocks(me, hidden, turned, first_step, True)
    out_below, out_above = move_y(out_up, 1), move_y(out_down, -1)

    all_packs, dpre = after((all_packs, dpre), out_up, out_down)
    in_later = in_blocks(me, all_packs, dpre, later_step, False)[0]
    hidden, turned = after((hidden, turned), in_later)
    out_later = out_blocks(me, hidden, turned, later_step, False)[0]

    def second_hop(later, from_below, from_above, move):
        up = (later[0].astype(F32) + from_below[0].astype(F32)).astype(BF16)
        down = (later[1].astype(F32) + from_above[0].astype(F32)).astype(BF16)
        return move(up, 1), move(down, -1), up, down

    in_below, in_above = after((in_below, in_above), out_later)
    in_hops = second_hop(in_later, in_below, in_above, move_x)
    out_below, out_above = after((out_below, out_above), in_hops[2:])
    out_hops = second_hop(out_later, out_below, out_above, move_y)

    def second_stage(total, move):
        keep, following, previous, far = total
        return keep, move(far, 2), move(following, 1), move(previous, -1)

    def add_up(parts):
        return parts[0] + parts[1].astype(F32) + parts[2].astype(F32) + parts[3].astype(F32)

    in_total = ring_total(me, in_later, in_hops[0], in_above, in_below, in_hops[1], True)
    in_parts = second_stage(in_total, move_y)
    out_hops = after(out_hops[:2], in_total)
    out_total = ring_total(me, out_later, out_hops[0], out_above, out_below, out_hops[1], False)
    out_parts = second_stage(out_total, move_x)

    sums = after(sums, out_total)
    ffn = sums[:routed].astype(F32)
    heavy = (score[:, None] * ffn).astype(BF16)
    grad_score = jnp.sum(cotan.astype(F32) * ffn, axis=1)
    place = picks[:, None] == jnp.arange(n_tok, dtype=jnp.int32)[None, :]
    grad_x = dot(place.astype(BF16), sums[routed:], ((0,), (0,))).astype(BF16)
    in_parts, out_parts = after((in_parts, out_parts), heavy, grad_x)
    grad_in = add_up(in_parts)
    grad_out = add_up(out_parts)
    return (heavy, grad_x, grad_score, grad_in, grad_out)


def solution(mesh):
    placed = (
        P(("ctx", "head"), None),
        P(("ctx", "head")),
        P(("ctx", "head")),
        P(("ctx", "head")),
        P(None, "head"),
        P("head", None),
        P(("ctx", "head"), None),
    )
    return jax.shard_map(
        on_device,
        mesh=mesh,
        in_specs=placed,
        out_specs=(
            P(("ctx", "head"), None),
            P(("ctx", "head"), None),
            P(("ctx", "head")),
            P("ctx", "head"),
            P("head", "ctx"),
        ),
        check_vma=False,
    )
```

profile of v0, /device:TPU:0, one launch (start us, length us, event | category | flops | bytes accessed | tf_op | source)
XLA Modules:
  0.0 165.1 jit_solution(5210035559080212423)
XLA Ops:
  7.9 3.2 %take_rows.1 = (bf16[2,128,2048]{2,1,0:T(8,128)(2,1)}, s32[2]{0:T(128)}) custom-call(s32[1]{0:T(128)S(6)} %copy.12.counts_ref, bf16[512,2048]{1,0:T(8,128)(2,1)} %tokens_ref.1, s32[1,128]{1,0:T(1,128)} %bitcast.13, f32[1,128]{1,0:T(1,128)} %bitcast.12, bf16[128,2048]{1,0:T(8,128)(2,1)} %cotan_ref.1), custom_call_target="tpu_custom_call" | custom-call | flops 1 | bytes 1 | tf_op jit(solution)/shard_map/take_rows/pallas_call | solution.py:74
  13.2 3.5 %hold_weights.1 = (bf16[2048,1024]{1,0:T(8,128)(2,1)S(1)}, bf16[1024,2048]{1,0:T(8,128)(2,1)S(1)}) custom-call(bf16[2048,1024]{1,0:T(8,128)(2,1)} %win_ref, bf16[1024,2048]{1,0:T(8,128)(2,1)} %wout_ref), custom_call_target="tpu_custom_call" | custom-call | flops 1 | bytes 1 | tf_op jit(solution)/shard_map/hold_weights/pallas_call | solution.py:156
  16.7 4.3 %hidden_units.3 = (bf16[256,1024]{1,0:T(8,128)(2,1)S(1)}, bf16[256,1024]{1,0:T(8,128)(2,1)S(1)}, bf16[256,2048]{1,0:T(8,128)(2,1)S(1)}) custom-call(bf16[2,128,2048]{2,1,0:T(8,128)(2,1)S(1)} %copy-done.1, bf16[2,128,2048]{2,1,0:T(8,128)(2,1)S(1)} %collective-permute-done.refs_1_, bf16[2048,1024]{1,0:T(8,128)(2,1)S(1)} %get-tuple-element.88.refs_2_.win_ref.refs_4_, ...), custom_call_target="tpu_custom_call" | custom-call | flops 1 | bytes 1 | tf_op jit(solution)/shard_map/hidden_units/pallas_call | solution.py:121
  22.0 6.3 %collective-permute-done.1.refs_0_.refs_2_ = bf16[2,128,2048]{2,1,0:T(8,128)(2,1)S(1)} collective-permute-done((bf16[2,128,2048]{2,1,0:T(8,128)(2,1)}, bf16[2,128,2048]{2,1,0:T(8,128)(2,1)S(1)}, u32[]{:S(2)}, u32[]{:S(2)}) %collective-permute-start.1) | collective-permute-done | bytes 1048608 | tf_op jit(solution)/shard_map/ppermute | solution.py:37
  30.2 3.3 %row_terms.2.refs_0_ = bf16[2,2,128,2048]{3,2,1,0:T(8,128)(2,1)S(1)} custom-call(bf16[256,1024]{1,0:T(8,128)(2,1)S(1)} %get-tuple-element.134.hidden_ref.refs_0_, bf16[256,1024]{1,0:T(8,128)(2,1)S(1)} %get-tuple-element.131.dpre_ref.refs_8_, bf16[2048,1024]{1,0:T(8,128)(2,1)S(1)} %get-tuple-element.88.refs_2_.win_ref.refs_4_, ...), custom_call_target="tpu_custom_call" | custom-call | flops 1 | bytes 1 | tf_op jit(solution)/shard_map/row_terms/pallas_call | solution.py:203
  33.6 4.3 %hidden_units.4 = (bf16[256,1024]{1,0:T(8,128)(2,1)S(1)}, bf16[256,1024]{1,0:T(8,128)(2,1)S(1)}, bf16[256,2048]{1,0:T(8,128)(2,1)S(1)}) custom-call(bf16[2,128,2048]{2,1,0:T(8,128)(2,1)S(1)} %collective-permute-done.1.refs_0_.refs_2_, bf16[2,128,2048]{2,1,0:T(8,128)(2,1)S(1)} %collective-permute-done.2.refs_1_.refs_3_, ...), custom_call_target="tpu_custom_call" | custom-call | flops 1 | bytes 1 | tf_op jit(solution)/shard_map/hidden_units/pallas_call | solution.py:121
  38.0 3.3 %row_terms.3.refs_1_ = bf16[2,2,128,2048]{3,2,1,0:T(8,128)(2,1)S(1)} custom-call(bf16[256,1024]{1,0:T(8,128)(2,1)S(1)} %get-tuple-element.135.hidden_ref.refs_1_, bf16[256,1024]{1,0:T(8,128)(2,1)S(1)} %get-tuple-element.132.dpre_ref.refs_9_, bf16[2048,1024]{1,0:T(8,128)(2,1)S(1)} %get-tuple-element.88.refs_2_.win_ref.refs_4_, ...), custom_call_target="tpu_custom_call" | custom-call | flops 1 | bytes 1 | tf_op jit(solution)/shard_map/row_terms/pallas_call | solution.py:203
  41.3 3.1 %collective-permute-done.3.refs_0_.refs_4_ = bf16[2,128,2048]{2,1,0:T(8,128)(2,1)S(1)} collective-permute-done((bf16[2,128,2048]{2,1,0:T(8,128)(2,1)S(1)}, bf16[2,128,2048]{2,1,0:T(8,128)(2,1)S(1)}, u32[]{:S(2)}, u32[]{:S(2)}) %collective-permute-start.3) | collective-permute-done | bytes 1048608 | tf_op jit(solution)/shard_map/ppermute | solution.py:37
  44.4 11.2 %collective-permute-done.4.refs_2_.refs_6_ = bf16[2,128,2048]{2,1,0:T(8,128)(2,1)S(1)} collective-permute-done((bf16[2,128,2048]{2,1,0:T(8,128)(2,1)S(1)}, bf16[2,128,2048]{2,1,0:T(8,128)(2,1)S(1)}, u32[]{:S(2)}, u32[]{:S(2)}) %collective-permute-start.4) | collective-permute-done | bytes 1048608 | tf_op jit(solution)/shard_map/ppermute | solution.py:37
  56.2 2.1 %collective-permute-done.5.refs_1_.refs_5_ = bf16[2,128,2048]{2,1,0:T(8,128)(2,1)S(1)} collective-permute-done((bf16[2,128,2048]{2,1,0:T(8,128)(2,1)S(1)}, bf16[2,128,2048]{2,1,0:T(8,128)(2,1)S(1)}, u32[]{:S(2)}, u32[]{:S(2)}) %collective-permute-start.5) | collective-permute-done | bytes 1048608 | tf_op jit(solution)/shard_map/ppermute | solution.py:41
  59.8 7.3 %hidden_units.5 = (bf16[512,1024]{1,0:T(8,128)(2,1)S(1)}, bf16[512,1024]{1,0:T(8,128)(2,1)S(1)}, bf16[512,2048]{1,0:T(8,128)(2,1)S(1)}) custom-call(bf16[2,128,2048]{2,1,0:T(8,128)(2,1)S(1)} %collective-permute-done.3.refs_0_.refs_4_, bf16[2,128,2048]{2,1,0:T(8,128)(2,1)S(1)} %collective-permute-done.5.refs_1_.refs_5_, ...), custom_call_target="tpu_custom_call" | custom-call | flops 1 | bytes 1 | tf_op jit(solution)/shard_map/hidden_units/pallas_call | solution.py:121
  68.4 7.7 %all_terms.1 = bf16[8,2,128,2048]{3,2,1,0:T(8,128)(2,1)} custom-call(s32[2]{0:T(128)S(1)} %copy-done.17, bf16[2,2,128,2048]{3,2,1,0:T(8,128)(2,1)S(1)} %row_terms.2.refs_0_, bf16[2,2,128,2048]{3,2,1,0:T(8,128)(2,1)S(1)} %row_terms.3.refs_1_, bf16[512,1024]{1,0:T(8,128)(2,1)S(1)} %get-tuple-element.136.refs_2_, ...), custom_call_target="tpu_custom_call" | custom-call | flops 1 | bytes 1 | tf_op jit(solution)/shard_map/all_terms/pallas_call | solution.py:244
  76.2 6.2 %weight_blocks.4 = (bf16[2,256,1024]{2,1,0:T(8,128)(2,1)S(1)}, bf16[2,256,1024]{2,1,0:T(8,128)(2,1)S(1)}) custom-call(s32[2]{0:T(128)S(1)} %copy-done.17, bf16[2,128,2048]{2,1,0:T(8,128)(2,1)} %get-tuple-element.123.refs_0_, bf16[2,128,2048]{2,1,0:T(8,128)(2,1)} %copy-done.2, bf16[2,128,2048]{2,1,0:T(8,128)(2,1)} %copy-done.3, ...), custom_call_target="tpu_custom_call" | custom-call | flops 1 | bytes 1 | tf_op jit(solution)/shard_map/weight_blocks/pallas_call | solution.py:347
  85.7 6.2 %weight_blocks.5 = (bf16[2,512,512]{2,1,0:T(8,128)(2,1)S(1)}, bf16[2,512,512]{2,1,0:T(8,128)(2,1)S(1)}) custom-call(s32[2]{0:T(128)S(1)} %copy-done.17, bf16[256,1024]{1,0:T(8,128)(2,1)} %copy-done.11, bf16[256,1024]{1,0:T(8,128)(2,1)} %copy-done.12, bf16[512,1024]{1,0:T(8,128)(2,1)} %copy-done, bf16[256,2048]{1,0:T(8,128)(2,1)} %copy-done.15, ...), custom_call_target="tpu_custom_call" | custom-call | flops 1 | bytes 1 | tf_op jit(solution)/shard_map/weight_blocks/pallas_call | solution.py:347
  95.3 6.1 %weight_blocks.6.later_ref = bf16[4,256,1024]{2,1,0:T(8,128)(2,1)S(1)} custom-call(s32[2]{0:T(128)S(1)} %copy-done.17, bf16[2,128,2048]{2,1,0:T(8,128)(2,1)} %get-tuple-element.123.refs_0_, bf16[2,128,2048]{2,1,0:T(8,128)(2,1)} %copy-done.2, bf16[2,128,2048]{2,1,0:T(8,128)(2,1)} %copy-done.3, bf16[2,128,2048]{2,1,0:T(8,128)(2,1)} %copy-done.4, ...), custom_call_target="tpu_custom_call" | custom-call | flops 1 | bytes 1 | tf_op jit(solution)/shard_map/weight_blocks/pallas_call | solution.py:347
  101.4 6.0 %weight_blocks.7.later_ref = bf16[4,512,512]{2,1,0:T(8,128)(2,1)S(1)} custom-call(s32[2]{0:T(128)S(1)} %copy-done.17, bf16[256,1024]{1,0:T(8,128)(2,1)} %copy-done.11, bf16[256,1024]{1,0:T(8,128)(2,1)} %copy-done.12, bf16[512,1024]{1,0:T(8,128)(2,1)} %copy-done, bf16[256,2048]{1,0:T(8,128)(2,1)} %copy-done.15, bf16[256,2048]{1,0:T(8,128)(2,1)} %copy-done.16, ...), custom_call_target="tpu_custom_call" | custom-call | flops 1 | bytes 1 | tf_op jit(solution)/shard_map/weight_blocks/pallas_call | solution.py:347
  109.3 3.0 %collective-permute-start.14 = (bf16[256,1024]{1,0:T(8,128)(2,1)S(1)}, bf16[256,1024]{1,0:T(8,128)(2,1)S(1)}, u32[]{:S(2)}, u32[]{:S(2)}) collective-permute-start(bf16[256,1024]{1,0:T(8,128)(2,1)S(1)} %get-tuple-element.165), channel_id=1, source_target_pairs={{0,96},{8,104},{16,112},{24,120},{32,0},{40,8},{48,16},{56,24},{64... | collective-permute-start | bytes 1572872 | tf_op jit(solution)/shard_map/ppermute | solution.py:27
  112.3 5.6 %collective-permute-done.7.b1 = bf16[2,512,512]{2,1,0:T(8,128)(2,1)S(1)} collective-permute-done((bf16[2,512,512]{2,1,0:T(8,128)(2,1)S(1)}, bf16[2,512,512]{2,1,0:T(8,128)(2,1)S(1)}, u32[]{:S(2)}, u32[]{:S(2)}) %collective-permute-start.7) | collective-permute-done | bytes 1048608 | tf_op jit(solution)/shard_map/ppermute | solution.py:32
  118.3 3.2 %collective-permute-start.12 = (bf16[512,512]{1,0:T(8,128)(2,1)S(1)}, bf16[512,512]{1,0:T(8,128)(2,1)S(1)}, u32[]{:S(2)}, u32[]{:S(2)}) collective-permute-start(bf16[512,512]{1,0:T(8,128)(2,1)S(1)} %get-tuple-element.163), channel_id=1, source_target_pairs={{0,24},{8,0},{16,8},{24,16},{32,56},{40,32},{48,40},{56,48},{64,88... | collective-permute-start | bytes 1572872 | tf_op jit(solution)/shard_map/ppermute | solution.py:32
  122.8 3.4 %collective-permute-done.13.b0 = bf16[256,1024]{1,0:T(8,128)(2,1)S(1)} collective-permute-done((bf16[256,1024]{1,0:T(8,128)(2,1)S(1)}, bf16[256,1024]{1,0:T(8,128)(2,1)S(1)}, u32[]{:S(2)}, u32[]{:S(2)}) %collective-permute-start.13) | collective-permute-done | bytes 524320 | tf_op jit(solution)/shard_map/ppermute | solution.py:27
  133.9 4.5 %collective-permute-done.11.b0 = bf16[512,512]{1,0:T(8,128)(2,1)S(1)} collective-permute-done((bf16[512,512]{1,0:T(8,128)(2,1)S(1)}, bf16[512,512]{1,0:T(8,128)(2,1)S(1)}, u32[]{:S(2)}, u32[]{:S(2)}) %collective-permute-start.11) | collective-permute-done | bytes 524320 | tf_op jit(solution)/shard_map/ppermute | solution.py:32
  140.0 3.1 %collective-permute-start.20 = (bf16[1024,128]{1,0:T(8,128)(2,1)S(1)}, bf16[1024,128]{1,0:T(8,128)(2,1)}, u32[]{:S(2)}, u32[]{:S(2)}) collective-permute-start(bf16[1024,128]{1,0:T(8,128)(2,1)S(1)} %get-tuple-element.152), channel_id=1, source_target_pairs={{0,96},{8,104},{16,112},{24,120},{32,0},{40,8},{48,16},{56,24},{64... | collective-permute-start | bytes 786440 | tf_op jit(solution)/shard_map/ppermute | solution.py:27
  143.2 3.3 %convolution_convert_fusion = bf16[512,2048]{1,0:T(8,128)(2,1)} fusion(bf16[256,2048]{1,0:T(8,128)(2,1)} %reduce-scatter.2.cloned.1.call-done, s32[128]{0:T(128)S(1)} %copy-done.21), kind=kOutput, calls=%fused_computation | convolution fusion | flops 269549568 | bytes 2621952 | tf_op jit(solution)/shard_map/dot_general | solution.py:45
  150.2 4.2 %collective-permute-done.18 = bf16[1024,128]{1,0:T(8,128)(2,1)S(1)} collective-permute-done((bf16[1024,128]{1,0:T(8,128)(2,1)S(1)}, bf16[1024,128]{1,0:T(8,128)(2,1)S(1)}, u32[]{:S(2)}, u32[]{:S(2)}) %collective-permute-start.18) | collective-permute-done | bytes 262176 | tf_op jit(solution)/shard_map/ppermute | solution.py:27
  (85 shorter events, 35.6 us)
Async XLA Ops:
  7.2 136.0 %reduce-scatter.2.cloned.1.call-start = ((), (), s32[]{:S(2)}) async-start(), calls=%async_computation.1 | async-start | bytes 9437184 | tf_op jit(solution)/shard_map/reduce_scatter | solution.py:430
  11.1 5.7 %collective-permute-start = (bf16[2,128,2048]{2,1,0:T(8,128)(2,1)}, bf16[2,128,2048]{2,1,0:T(8,128)(2,1)S(1)}, u32[]{:S(2)}, u32[]{:S(2)}) collective-permute-start(bf16[2,128,2048]{2,1,0:T(8,128)(2,1)} %get-tuple-element.123.refs_0_), channel_id=1, source_target_pairs={{0,1},{1,0},{2,3},{3,2},{4,5},{5,4},{6,7},{7,6},{8,9},{9,8},{10,11... | collective-permute-start | bytes 3145736 | tf_op jit(solution)/shard_map/ppermute | solution.py:41
  11.1 17.2 %collective-permute-start.1 = (bf16[2,128,2048]{2,1,0:T(8,128)(2,1)}, bf16[2,128,2048]{2,1,0:T(8,128)(2,1)S(1)}, u32[]{:S(2)}, u32[]{:S(2)}) collective-permute-start(bf16[2,128,2048]{2,1,0:T(8,128)(2,1)} %get-tuple-element.123.refs_0_), channel_id=1, source_target_pairs={{0,2},{1,7},{2,4},{3,1},{4,6},{5,3},{6,0},{7,5},{8,10},{9,15},{10,... | collective-permute-start | bytes 3145736 | tf_op jit(solution)/shard_map/ppermute | solution.py:37
  28.3 5.2 %collective-permute-start.2 = (bf16[2,128,2048]{2,1,0:T(8,128)(2,1)S(1)}, bf16[2,128,2048]{2,1,0:T(8,128)(2,1)S(1)}, u32[]{:S(2)}, u32[]{:S(2)}) collective-permute-start(bf16[2,128,2048]{2,1,0:T(8,128)(2,1)S(1)} %collective-permute-done.1.refs_0_.refs_2_), channel_id=1, source_target_pairs={{0,1},{1,0},{2,3},{3,2},{4,5},{5,4},{6,7},{7,6},{8,9},{9,8},{10,11... | collective-permute-start | bytes 3145736 | tf_op jit(solution)/shard_map/ppermute | solution.py:41
  28.3 16.1 %collective-permute-start.3 = (bf16[2,128,2048]{2,1,0:T(8,128)(2,1)S(1)}, bf16[2,128,2048]{2,1,0:T(8,128)(2,1)S(1)}, u32[]{:S(2)}, u32[]{:S(2)}) collective-permute-start(bf16[2,128,2048]{2,1,0:T(8,128)(2,1)S(1)} %collective-permute-done.refs_1_), channel_id=1, source_target_pairs={{0,2},{1,7},{2,4},{3,1},{4,6},{5,3},{6,0},{7,5},{8,10},{9,15},{10,... | collective-permute-start | bytes 3145736 | tf_op jit(solution)/shard_map/ppermute | solution.py:37
  28.4 27.2 %collective-permute-start.4 = (bf16[2,128,2048]{2,1,0:T(8,128)(2,1)S(1)}, bf16[2,128,2048]{2,1,0:T(8,128)(2,1)S(1)}, u32[]{:S(2)}, u32[]{:S(2)}) collective-permute-start(bf16[2,128,2048]{2,1,0:T(8,128)(2,1)S(1)} %collective-permute-done.1.refs_0_.refs_2_), channel_id=1, source_target_pairs={{0,2},{1,7},{2,4},{3,1},{4,6},{5,3},{6,0},{7,5},{8,10},{9,15},{10,... | collective-permute-start | bytes 3145736 | tf_op jit(solution)/shard_map/ppermute | solution.py:37
  44.4 22.7 %copy-start.5 = (bf16[2,128,2048]{2,1,0:T(8,128)(2,1)}, bf16[2,128,2048]{2,1,0:T(8,128)(2,1)S(1)}, u32[]{:S(2)}) copy-start(bf16[2,128,2048]{2,1,0:T(8,128)(2,1)S(1)} %collective-permute-done.3.refs_0_.refs_4_) | copy-start | bytes 3145732
  55.6 12.8 %copy-start.17 = (s32[2]{0:T(128)S(1)}, s32[2]{0:T(128)}, u32[]{:S(2)}) copy-start(s32[2]{0:T(128)} %get-tuple-element.84.me_ref) | copy-start | bytes 28
  55.7 2.7 %collective-permute-start.5 = (bf16[2,128,2048]{2,1,0:T(8,128)(2,1)S(1)}, bf16[2,128,2048]{2,1,0:T(8,128)(2,1)S(1)}, u32[]{:S(2)}, u32[]{:S(2)}) collective-permute-start(bf16[2,128,2048]{2,1,0:T(8,128)(2,1)S(1)} %collective-permute-done.3.refs_0_.refs_4_), channel_id=1, source_target_pairs={{0,1},{1,0},{2,3},{3,2},{4,5},{5,4},{6,7},{7,6},{8,9},{9,8},{10,11... | collective-permute-start | bytes 3145736 | tf_op jit(solution)/shard_map/ppermute | solution.py:41
  55.7 4.2 %collective-permute-start.6 = (bf16[2,128,2048]{2,1,0:T(8,128)(2,1)S(1)}, bf16[2,128,2048]{2,1,0:T(8,128)(2,1)S(1)}, u32[]{:S(2)}, u32[]{:S(2)}) collective-permute-start(bf16[2,128,2048]{2,1,0:T(8,128)(2,1)S(1)} %collective-permute-done.4.refs_2_.refs_6_), channel_id=1, source_target_pairs={{0,1},{1,0},{2,3},{3,2},{4,5},{5,4},{6,7},{7,6},{8,9},{9,8},{10,11... | collective-permute-start | bytes 3145736 | tf_op jit(solution)/shard_map/ppermute | solution.py:41
  82.4 26.5 %collective-permute-start.9 = (bf16[2,256,1024]{2,1,0:T(8,128)(2,1)S(1)}, bf16[2,256,1024]{2,1,0:T(8,128)(2,1)S(1)}, u32[]{:S(2)}, u32[]{:S(2)}) collective-permute-start(bf16[2,256,1024]{2,1,0:T(8,128)(2,1)S(1)} %get-tuple-element.113), channel_id=1, source_target_pairs={{0,32},{8,40},{16,48},{24,56},{32,64},{40,72},{48,80},{56,88},{64,... | collective-permute-start | bytes 3145736 | tf_op jit(solution)/shard_map/ppermute | solution.py:27
  84.0 24.9 %collective-permute-start.10 = (bf16[2,256,1024]{2,1,0:T(8,128)(2,1)S(1)}, bf16[2,256,1024]{2,1,0:T(8,128)(2,1)S(1)}, u32[]{:S(2)}, u32[]{:S(2)}) collective-permute-start(bf16[2,256,1024]{2,1,0:T(8,128)(2,1)S(1)} %get-tuple-element.114), channel_id=1, source_target_pairs={{0,96},{8,104},{16,112},{24,120},{32,0},{40,8},{48,16},{56,24},{64... | collective-permute-start | bytes 3145736 | tf_op jit(solution)/shard_map/ppermute | solution.py:27
  91.9 26.0 %collective-permute-start.7 = (bf16[2,512,512]{2,1,0:T(8,128)(2,1)S(1)}, bf16[2,512,512]{2,1,0:T(8,128)(2,1)S(1)}, u32[]{:S(2)}, u32[]{:S(2)}) collective-permute-start(bf16[2,512,512]{2,1,0:T(8,128)(2,1)S(1)} %get-tuple-element.121), channel_id=1, source_target_pairs={{0,8},{8,16},{16,24},{24,0},{32,40},{40,48},{48,56},{56,32},{64,72... | collective-permute-start | bytes 3145736 | tf_op jit(solution)/shard_map/ppermute | solution.py:32
  93.6 24.4 %collective-permute-start.8 = (bf16[2,512,512]{2,1,0:T(8,128)(2,1)S(1)}, bf16[2,512,512]{2,1,0:T(8,128)(2,1)S(1)}, u32[]{:S(2)}, u32[]{:S(2)}) collective-permute-start(bf16[2,512,512]{2,1,0:T(8,128)(2,1)S(1)} %get-tuple-element.122), channel_id=1, source_target_pairs={{0,24},{8,0},{16,8},{24,16},{32,56},{40,32},{48,40},{56,48},{64,88... | collective-permute-start | bytes 3145736 | tf_op jit(solution)/shard_map/ppermute | solution.py:32
  109.3 13.5 %collective-permute-start.14 = (bf16[256,1024]{1,0:T(8,128)(2,1)S(1)}, bf16[256,1024]{1,0:T(8,128)(2,1)S(1)}, u32[]{:S(2)}, u32[]{:S(2)}) collective-permute-start(bf16[256,1024]{1,0:T(8,128)(2,1)S(1)} %get-tuple-element.165), channel_id=1, source_target_pairs={{0,96},{8,104},{16,112},{24,120},{32,0},{40,8},{48,16},{56,24},{64... | collective-permute-start | bytes 1572872 | tf_op jit(solution)/shard_map/ppermute | solution.py:27
  112.3 13.9 %collective-permute-start.13 = (bf16[256,1024]{1,0:T(8,128)(2,1)S(1)}, bf16[256,1024]{1,0:T(8,128)(2,1)S(1)}, u32[]{:S(2)}, u32[]{:S(2)}) collective-permute-start(bf16[256,1024]{1,0:T(8,128)(2,1)S(1)} %get-tuple-element.166), channel_id=1, source_target_pairs={{0,32},{8,40},{16,48},{24,56},{32,64},{40,72},{48,80},{56,88},{64,... | collective-permute-start | bytes 1572872 | tf_op jit(solution)/shard_map/ppermute | solution.py:27
  118.3 15.6 %collective-permute-start.12 = (bf16[512,512]{1,0:T(8,128)(2,1)S(1)}, bf16[512,512]{1,0:T(8,128)(2,1)S(1)}, u32[]{:S(2)}, u32[]{:S(2)}) collective-permute-start(bf16[512,512]{1,0:T(8,128)(2,1)S(1)} %get-tuple-element.163), channel_id=1, source_target_pairs={{0,24},{8,0},{16,8},{24,16},{32,56},{40,32},{48,40},{56,48},{64,88... | collective-permute-start | bytes 1572872 | tf_op jit(solution)/shard_map/ppermute | solution.py:32
  121.5 16.9 %collective-permute-start.11 = (bf16[512,512]{1,0:T(8,128)(2,1)S(1)}, bf16[512,512]{1,0:T(8,128)(2,1)S(1)}, u32[]{:S(2)}, u32[]{:S(2)}) collective-permute-start(bf16[512,512]{1,0:T(8,128)(2,1)S(1)} %get-tuple-element.164), channel_id=1, source_target_pairs={{0,8},{8,16},{16,24},{24,0},{32,40},{40,48},{48,56},{56,32},{64,72... | collective-permute-start | bytes 1572872 | tf_op jit(solution)/shard_map/ppermute | solution.py:32
  127.5 19.0 %collective-permute-start.16 = (bf16[128,1024]{1,0:T(8,128)(2,1)S(1)}, bf16[128,1024]{1,0:T(8,128)(2,1)S(1)}, u32[]{:S(2)}, u32[]{:S(2)}) collective-permute-start(bf16[128,1024]{1,0:T(8,128)(2,1)S(1)} %get-tuple-element.145), channel_id=1, source_target_pairs={{0,8},{8,16},{16,24},{24,0},{32,40},{40,48},{48,56},{56,32},{64,72... | collective-permute-start | bytes 786440 | tf_op jit(solution)/shard_map/ppermute | solution.py:32
  129.1 20.8 %collective-permute-start.17 = (bf16[128,1024]{1,0:T(8,128)(2,1)S(1)}, bf16[128,1024]{1,0:T(8,128)(2,1)}, u32[]{:S(2)}, u32[]{:S(2)}) collective-permute-start(bf16[128,1024]{1,0:T(8,128)(2,1)S(1)} %get-tuple-element.146), channel_id=1, source_target_pairs={{0,24},{8,0},{16,8},{24,16},{32,56},{40,32},{48,40},{56,48},{64,88... | collective-permute-start | bytes 786440 | tf_op jit(solution)/shard_map/ppermute | solution.py:32
  130.8 19.2 %collective-permute-start.15 = (bf16[128,1024]{1,0:T(8,128)(2,1)S(1)}, bf16[128,1024]{1,0:T(8,128)(2,1)}, u32[]{:S(2)}, u32[]{:S(2)}) collective-permute-start(bf16[128,1024]{1,0:T(8,128)(2,1)S(1)} %get-tuple-element.147), channel_id=1, source_target_pairs={{0,16},{8,24},{16,0},{24,8},{32,48},{40,56},{48,32},{56,40},{64,80... | collective-permute-start | bytes 786440 | tf_op jit(solution)/shard_map/ppermute | solution.py:32
  139.9 10.3 %collective-permute-start.19 = (bf16[1024,128]{1,0:T(8,128)(2,1)S(1)}, bf16[1024,128]{1,0:T(8,128)(2,1)}, u32[]{:S(2)}, u32[]{:S(2)}) collective-permute-start(bf16[1024,128]{1,0:T(8,128)(2,1)S(1)} %get-tuple-element.151), channel_id=1, source_target_pairs={{0,32},{8,40},{16,48},{24,56},{32,64},{40,72},{48,80},{56,88},{64,... | collective-permute-start | bytes 786440 | tf_op jit(solution)/shard_map/ppermute | solution.py:27
  140.0 10.1 %collective-permute-start.20 = (bf16[1024,128]{1,0:T(8,128)(2,1)S(1)}, bf16[1024,128]{1,0:T(8,128)(2,1)}, u32[]{:S(2)}, u32[]{:S(2)}) collective-permute-start(bf16[1024,128]{1,0:T(8,128)(2,1)S(1)} %get-tuple-element.152), channel_id=1, source_target_pairs={{0,96},{8,104},{16,112},{24,120},{32,0},{40,8},{48,16},{56,24},{64... | collective-permute-start | bytes 786440 | tf_op jit(solution)/shard_map/ppermute | solution.py:27
  146.5 7.9 %collective-permute-start.18 = (bf16[1024,128]{1,0:T(8,128)(2,1)S(1)}, bf16[1024,128]{1,0:T(8,128)(2,1)S(1)}, u32[]{:S(2)}, u32[]{:S(2)}) collective-permute-start(bf16[1024,128]{1,0:T(8,128)(2,1)S(1)} %get-tuple-element.153), channel_id=1, source_target_pairs={{0,64},{8,72},{16,80},{24,88},{32,96},{40,104},{48,112},{56,120},{... | collective-permute-start | bytes 786440 | tf_op jit(solution)/shard_map/ppermute | solution.py:27
  (20 other events, 132.3 us)
Sparse Core Ops, SparseCore 0:
  76.3 52.2 reduce-scatter.1
where the time goes:
time: 166 us; the launch traced here: 165 us
  Pallas kernels  64.1 us (39%)
  waiting for transfers between devices  46.1 us (28%)
  starting transfers between devices  28.1 us (17%)
  between operations  15 us (9%)
  other arithmetic  6.17 us (4%)
  matrix products  3.27 us (2%)
  local copies, waits for them, and re-layouts  2.35 us (1%)
    pallas_call x4, Pallas kernels, blocks_call(): pl.pallas_call(body, grid_spec=pltpu.PrefetchScalarGridSpec(num_scalar_pr...  24.5 us
    ppermute x3, waiting for transfers between devices, move_lane(): return lax.ppermute(v, 'head', perm)  20.6 us
    pallas_call x3, Pallas kernels, hidden_units(): pl.pallas_call(body, grid=(SIDE,), in_specs=[whole(a) for a in packs] + [...  15.9 us
    ppermute x7, starting transfers between devices, move_y(): return lax.ppermute(v, 'ctx', perm)  11.9 us
    ppermute x7, starting transfers between devices, move_x(): return lax.ppermute(v, 'ctx', perm)  11.5 us
    ppermute x7, waiting for transfers between devices, move_y(): return lax.ppermute(v, 'ctx', perm)  11.3 us
    ppermute x7, waiting for transfers between devices, move_x(): return lax.ppermute(v, 'ctx', perm)  10.5 us
    pallas_call x1, Pallas kernels, all_terms(): pl.pallas_call(body, grid_spec=pltpu.PrefetchScalarGridSpec(num_scalar_pr...  7.72 us
  transfers between devices with their start and end apart: 22, of which 13 were waited for; matrix products, arithmetic and copies ran while one was open for 3% of the time, Pallas kernels for 28%

commit v1 on v0

--- a/solution.py
+++ b/solution.py
@@ -169,37 +169,22 @@
     return pltpu.with_memory_space_constraint(w, pltpu.VMEM)
 
 
-def in_hbm(arrays):
-    return [pltpu.with_memory_space_constraint(a, pltpu.HBM) for a in arrays]
-
-
-def owners(head):
-    chip, core = head // 2, lax.rem(head, 2)
-    back = 1 + 2 * core
-    here, behind = chip, lax.rem(chip + SIDE - back, SIDE)
-    ahead, far = lax.rem(chip + back, SIDE), lax.rem(chip + 2, SIDE)
-    rest = 1 - core
-    return [
-        here * 2 + core, here * 2 + rest,
-        behind * 2 + core, ahead * 2 + rest,
-        behind * 2 + rest, ahead * 2 + core,
-        far * 2 + core, far * 2 + rest,
-    ]
-
-
-def row_terms(hidden, dpre, w_in, w_out, piece):
+def row_terms(hidden, dpre, w_in, w_out, piece, groups, held_terms=()):
     count, hid = hidden.shape
     width = w_in.shape[0]
-    n = count // piece
+    n = count // (2 * piece)
     tile = width // SIDE
 
-    def body(hidden_ref, dpre_ref, win_ref, wout_ref, out_ref):
+    def body(hidden_ref, dpre_ref, win_ref, wout_ref, *refs):
+        outs = refs[len(held_terms) :]
         ffn = dot(hidden_ref[...], wout_ref[...], ((1,), (0,))).astype(BF16)
         dx = dot(dpre_ref[...], win_ref[...], ((1,), (1,))).astype(BF16)
-        for s, v in enumerate((ffn, dx)):
+        for h in range(2):
             for k in range(n):
-                out_ref[k, s] = v[k * piece : (k + 1) * piece]
-
+                for s, v in enumerate((ffn, dx)):
+                    outs[h][k, s] = v[(h * n + k) * piece : (h * n + k + 1) * piece]
+
+    first = groups - 1 if held_terms else 0
     return pl.pallas_call(
         body,
         grid=(SIDE,),
@@ -208,58 +193,15 @@
             whole(dpre),
             pl.BlockSpec((tile, hid), lambda j: (j, 0)),
             pl.BlockSpec((hid, tile), lambda j: (0, j)),
-        ],
-        out_specs=pl.BlockSpec((n, 2, piece, tile), lambda j: (0, 0, 0, j)),
-        out_shape=jax.ShapeDtypeStruct((n, 2, piece, width), BF16),
-        compiler_params=params(8),
+        ]
+        + [pl.BlockSpec(memory_space=pl.ANY)] * len(held_terms),
+        out_specs=[pl.BlockSpec((n, 2, piece, tile), lambda j: (first, 0, 0, j))] * 2,
+        out_shape=[jax.ShapeDtypeStruct((groups, 2, piece, width), BF16)] * 2,
+        input_output_aliases={4 + i: i for i in range(len(held_terms))},
+        compiler_params=params(6 + count // 64),
         cost_estimate=LITTLE,
         name="row_terms",
-    )(hidden, dpre, held(w_in), held(w_out))
-
-
-def all_terms(me, earlier, hidden, dpre, w_in, w_out, piece):
-    count, hid = hidden.shape
-    width = w_in.shape[0]
-    n = count // piece
-    tile = width // SIDE
-    total = n + sum(a.shape[0] for a in earlier)
-
-    def body(me_ref, *refs):
-        hidden_ref, dpre_ref, win_ref, wout_ref, out_ref = refs[len(earlier) :]
-        to = owners(me_ref[1])
-        at = 0
-        for ref in refs[: len(earlier)]:
-            for k in range(ref.shape[0]):
-                out_ref[to[at]] = ref[k]
-                at += 1
-        ffn = dot(hidden_ref[...], wout_ref[...], ((1,), (0,))).astype(BF16)
-        dx = dot(dpre_ref[...], win_ref[...], ((1,), (1,))).astype(BF16)
-        for k in range(n):
-            for s, v in enumerate((ffn, dx)):
-                out_ref[to[at + k], s] = v[k * piece : (k + 1) * piece]
-
-    def terms(a):
-        return pl.BlockSpec((a.shape[0], 2, piece, tile), lambda j, h: (0, 0, 0, j))
-
-    return pl.pallas_call(
-        body,
-        grid_spec=pltpu.PrefetchScalarGridSpec(
-            num_scalar_prefetch=1,
-            grid=(SIDE,),
-            in_specs=[terms(a) for a in earlier]
-            + [
-                whole(hidden),
-                whole(dpre),
-                pl.BlockSpec((tile, hid), lambda j, h: (j, 0)),
-                pl.BlockSpec((hid, tile), lambda j, h: (0, j)),
-            ],
-            out_specs=pl.BlockSpec((total, 2, piece, tile), lambda j, h: (0, 0, 0, j)),
-        ),
-        out_shape=pltpu.HBM((total, 2, piece, width), BF16),
-        compiler_params=params(14),
-        cost_estimate=LITTLE,
-        name="all_terms",
-    )(me, *earlier, hidden, dpre, held(w_in), held(w_out))
+    )(hidden, dpre, held(w_in), held(w_out), *held_terms)
 
 
 def first_step(i):
@@ -301,7 +243,7 @@
         return (0, 0, 2 * lax.rem(me_ref[0] // SIDE + place, SIDE) + half)
 
     return blocks_call(body, me, [pl.BlockSpec((1, piece, size), columns)] * n + [whole(a) for a in dpre],
-                       in_hbm(packs + dpre), (size, hid), split, n * piece)
+                       packs + dpre, (size, hid), split, n * piece)
 
 
 def out_blocks(me, hidden, turned, order, split):
@@ -334,7 +276,7 @@
 
     specs = [pl.BlockSpec((a.shape[0], hid // 2), units) for a in hidden]
     specs += [pl.BlockSpec((a.shape[0], quarter), columns) for a in turned]
-    return blocks_call(body, me, specs, in_hbm(hidden + turned), (hid // 2, quarter), split, count)
+    return blocks_call(body, me, specs, hidden + turned, (hid // 2, quarter), split, count)
 
 
 def blocks_call(body, me, specs, args, block, split, count):
@@ -415,32 +357,41 @@
     own = hidden_units(own_packs, w_in, w_out)
 
     near_other = move_lane(own_other, 1)
+    own_terms = row_terms(own[0], own[1], w_in, w_out, routed, 1)
+    own_got = swap_core(own_terms[1])
     near_mine = after(near_mine, own)
     far_mine = move_lane(near_mine, 1)
-    near_packs = [near_mine, swap_core(near_mine)]
+    near_packs = [near_mine, near_other, swap_core(near_mine), swap_core(near_other)]
+    near_packs, own_got = after((near_packs, own_got), own)
     near = hidden_units(near_packs, w_in, w_out)
-    own_terms = row_terms(own[0], own[1], w_in, w_out, routed)
-    near_terms = row_terms(near[0], near[1], w_in, w_out, routed)
-
-    near_other, far_mine = after((near_other, far_mine), near, own_terms, near_terms)
-    last_packs = [near_other, swap_core(near_other), far_mine, swap_core(far_mine)]
-    last = hidden_units(last_packs, w_in, w_out)
-    terms = all_terms(me, [own_terms, near_terms], last[0], last[1], w_in, w_out, routed)
-    width = tokens.shape[1]
-    sums = lax.psum_scatter(terms.reshape(-1, width), "head", scatter_dimension=0, tiled=True)
-
-    all_packs = own_packs + near_packs + last_packs
-    hidden, dpre, turned = ([u[i] for u in (own, near, last)] for i in range(3))
-    all_packs, dpre = after((all_packs, dpre), terms)
+
+    near_terms = row_terms(near[0], near[1], w_in, w_out, routed, 3)
+    far_mine = after(far_mine, near_terms)
+    far_packs = [far_mine, swap_core(far_mine)]
+    far = hidden_units(far_packs, w_in, w_out)
+    last_terms = row_terms(far[0], far[1], w_in, w_out, routed, 3, near_terms)
+    last_got = swap_core(last_terms[1])
+
+    all_packs = own_packs + near_packs + far_packs
+    hidden, dpre, turned = ([u[i] for u in (own, near, far)] for i in range(3))
+    all_packs, dpre = after((all_packs, dpre), last_terms)
     in_up, in_down = in_blocks(me, all_packs, dpre, first_step, True)
     in_below, in_above = move_x(in_up, 1), move_x(in_down, -1)
-    hidden, turned = after((hidden, turned), in_up, in_down)
+
+    last_got = after(last_got, in_up, in_down)
+    to_far = (last_terms[0][2].astype(F32) + last_got[2].astype(F32)).astype(BF16)
+    z_far = move_lane(to_far, -1)
+
+    hidden, turned = after((hidden, turned), to_far)
     out_up, out_down = out_blocks(me, hidden, turned, first_step, True)
     out_below, out_above = move_y(out_up, 1), move_y(out_down, -1)
-
     all_packs, dpre = after((all_packs, dpre), out_up, out_down)
     in_later = in_blocks(me, all_packs, dpre, later_step, False)[0]
-    hidden, turned = after((hidden, turned), in_later)
+    z_far = after(z_far, in_later)
+    passed = jnp.pad(z_far.astype(F32)[None], ((0, 1), (0, 0), (0, 0), (0, 0)))
+    to_near = (last_terms[0][:2].astype(F32) + last_got[:2].astype(F32) + passed).astype(BF16)
+    z_near = move_lane(to_near, -1)
+    hidden, turned = after((hidden, turned), to_near)
     out_later = out_blocks(me, hidden, turned, later_step, False)[0]
 
     def second_hop(later, from_below, from_above, move):
@@ -448,10 +399,12 @@
         down = (later[1].astype(F32) + from_above[0].astype(F32)).astype(BF16)
         return move(up, 1), move(down, -1), up, down
 
-    in_below, in_above = after((in_below, in_above), out_later)
+    in_below, in_above, out_below, out_above = after((in_below, in_above, out_below, out_above), out_later)
     in_hops = second_hop(in_later, in_below, in_above, move_x)
-    out_below, out_above = after((out_below, out_above), in_hops[2:])
     out_hops = second_hop(out_later, out_below, out_above, move_y)
+    in_hops, out_hops = lax.optimization_barrier((in_hops[:2], out_hops[:2]))
+    z_near = after(z_near, in_hops, out_hops)
+    z_other = swap_core(z_near[1])
 
     def second_stage(total, move):
         keep, following, previous, far = total
@@ -461,17 +414,19 @@
         return parts[0] + parts[1].astype(F32) + parts[2].astype(F32) + parts[3].astype(F32)
 
     in_total = ring_total(me, in_later, in_hops[0], in_above, in_below, in_hops[1], True)
+    out_total = ring_total(me, out_later, out_hops[0], out_above, out_below, out_hops[1], False)
+    in_total, out_total = after((in_total, out_total), z_other)
     in_parts = second_stage(in_total, move_y)
-    out_hops = after(out_hops[:2], in_total)
-    out_total = ring_total(me, out_later, out_hops[0], out_above, out_below, out_hops[1], False)
     out_parts = second_stage(out_total, move_x)
 
-    sums = after(sums, out_total)
-    ffn = sums[:routed].astype(F32)
+    back = (
+        own_terms[0][0].astype(F32) + own_got[0].astype(F32) + z_near[0].astype(F32) + z_other.astype(F32)
+    ).astype(BF16)
+    ffn = back[0].astype(F32)
     heavy = (score[:, None] * ffn).astype(BF16)
     grad_score = jnp.sum(cotan.astype(F32) * ffn, axis=1)
     place = picks[:, None] == jnp.arange(n_tok, dtype=jnp.int32)[None, :]
-    grad_x = dot(place.astype(BF16), sums[routed:], ((0,), (0,))).astype(BF16)
+    grad_x = dot(place.astype(BF16), back[1], ((0,), (0,))).astype(BF16)
     in_parts, out_parts = after((in_parts, out_parts), heavy, grad_x)
     grad_in = add_up(in_parts)
     grad_out = add_up(out_parts)

time: 166 us -> 143 us (0.86)
  the two profiles are of different devices: /device:TPU:0 before, /device:TPU:70 now
where the time goes in v1:
time: 143 us
  Pallas kernels  55.7 us (39%)
  waiting for transfers between devices  50.8 us (36%)
  starting transfers between devices  26.6 us (19%)
  other arithmetic  6.14 us (4%)
  matrix products  2.15 us (2%)
  between operations  1.55 us (1%)
    ppermute x7, waiting for transfers between devices, move_y(): return lax.ppermute(v, 'ctx', perm)  18.2 us
    pallas_call x4, Pallas kernels, blocks_call(): pl.pallas_call(body, grid_spec=pltpu.PrefetchScalarGridSpec(num_scalar_pr...  18 us
    ppermute x7, waiting for transfers between devices, move_x(): return lax.ppermute(v, 'ctx', perm)  17.3 us
    pallas_call x3, Pallas kernels, hidden_units(): pl.pallas_call(body, grid=(SIDE,), in_specs=[whole(a) for a in packs] + [...  15.9 us
    pallas_call x3, Pallas kernels, row_terms(): pl.pallas_call(body, grid=(SIDE,), in_specs=[whole(hidden), whole(dpre),...  12.3 us
    ppermute x5, waiting for transfers between devices, move_lane(): return lax.ppermute(v, 'head', perm)  10.2 us
    ppermute x7, starting transfers between devices, move_y(): return lax.ppermute(v, 'ctx', perm)  9.85 us
    ppermute x5, starting transfers between devices, move_lane(): return lax.ppermute(v, 'head', perm)  7.92 us
  transfers between devices with their start and end apart: 26, of which 17 were waited for; matrix products, arithmetic and copies ran while one was open for 4% of the time, Pallas kernels for 31%

profile of v1, /device:TPU:70, one launch (start us, length us, event | category | flops | bytes accessed | tf_op | source)
XLA Modules:
  0.0 143.0 jit_solution(18136475575350822010)
XLA Ops:
  1.3 3.2 %take_rows.1 = (bf16[2,128,2048]{2,1,0:T(8,128)(2,1)}, s32[2]{0:T(128)}) custom-call(s32[1]{0:T(128)S(6)} %copy.16.counts_ref, bf16[512,2048]{1,0:T(8,128)(2,1)} %tokens_ref.1, s32[1,128]{1,0:T(1,128)} %bitcast.31, f32[1,128]{1,0:T(1,128)} %bitcast.30, bf16[128,2048]{1,0:T(8,128)(2,1)} %cotan_ref.1), custom_call_target="tpu_custom_call" | custom-call | flops 1 | bytes 1 | tf_op jit(solution)/shard_map/take_rows/pallas_call | solution.py:74
  9.0 3.5 %hold_weights.1 = (bf16[2048,1024]{1,0:T(8,128)(2,1)S(1)}, bf16[1024,2048]{1,0:T(8,128)(2,1)S(1)}) custom-call(bf16[2048,1024]{1,0:T(8,128)(2,1)} %win_ref, bf16[1024,2048]{1,0:T(8,128)(2,1)} %wout_ref), custom_call_target="tpu_custom_call" | custom-call | flops 1 | bytes 1 | tf_op jit(solution)/shard_map/hold_weights/pallas_call | solution.py:156
  12.5 4.3 %hidden_units.3 = (bf16[256,1024]{1,0:T(8,128)(2,1)S(1)}, bf16[256,1024]{1,0:T(8,128)(2,1)S(1)}, bf16[256,2048]{1,0:T(8,128)(2,1)S(1)}) custom-call(bf16[2,128,2048]{2,1,0:T(8,128)(2,1)S(1)} %copy-done, bf16[2,128,2048]{2,1,0:T(8,128)(2,1)S(1)} %collective-permute-done.refs_1_, bf16[2048,1024]{1,0:T(8,128)(2,1)S(1)} %get-tuple-element.109.refs_2_.win_ref.refs_4_, ...), custom_call_target="tpu_custom_call" | custom-call | flops 1 | bytes 1 | tf_op jit(solution)/shard_map/hidden_units/pallas_call | solution.py:121
  16.9 3.4 %row_terms.3 = (bf16[1,2,128,2048]{3,2,1,0:T(8,128)(2,1)S(1)}, bf16[1,2,128,2048]{3,2,1,0:T(8,128)(2,1)S(1)}) custom-call(bf16[256,1024]{1,0:T(8,128)(2,1)S(1)} %get-tuple-element.168.hidden_ref.refs_0_, bf16[256,1024]{1,0:T(8,128)(2,1)S(1)} %get-tuple-element.164.dpre_ref.refs_8_, bf16[2048,1024]{1,0:T(8,128)(2,1)S(1)} %get-tuple-element.109.refs_2_.win_ref.refs_4_, ...), custom_call_target="tpu_custom_call" | custom-call | flops 1 | bytes 1 | tf_op jit(solution)/shard_map/row_terms/pallas_call | solution.py:188
  20.8 10.0 %collective-permute-done.2.refs_1_.refs_3_ = bf16[2,128,2048]{2,1,0:T(8,128)(2,1)S(1)} collective-permute-done((bf16[2,128,2048]{2,1,0:T(8,128)(2,1)S(1)}, bf16[2,128,2048]{2,1,0:T(8,128)(2,1)S(1)}, u32[]{:S(2)}, u32[]{:S(2)}) %collective-permute-start.2) | collective-permute-done | bytes 1048608 | tf_op jit(solution)/shard_map/ppermute | solution.py:37
  33.5 7.3 %hidden_units.4 = (bf16[512,1024]{1,0:T(8,128)(2,1)S(1)}, bf16[512,1024]{1,0:T(8,128)(2,1)S(1)}, bf16[512,2048]{1,0:T(8,128)(2,1)S(1)}) custom-call(bf16[2,128,2048]{2,1,0:T(8,128)(2,1)S(1)} %collective-permute-done.1.refs_0_.refs_2_, bf16[2,128,2048]{2,1,0:T(8,128)(2,1)S(1)} %collective-permute-done.2.refs_1_.refs_3_, ...), custom_call_target="tpu_custom_call" | custom-call | flops 1 | bytes 1 | tf_op jit(solution)/shard_map/hidden_units/pallas_call | solution.py:121
  40.8 5.6 %row_terms.4 = (bf16[3,2,128,2048]{3,2,1,0:T(8,128)(2,1)S(1)}, bf16[3,2,128,2048]{3,2,1,0:T(8,128)(2,1)S(1)}) custom-call(bf16[512,1024]{1,0:T(8,128)(2,1)S(1)} %get-tuple-element.169.hidden_ref.refs_1_, bf16[512,1024]{1,0:T(8,128)(2,1)S(1)} %get-tuple-element.165.dpre_ref.refs_9_, bf16[2048,1024]{1,0:T(8,128)(2,1)S(1)} %get-tuple-element.109.refs_2_.win_ref.refs_4_, ...), custom_call_target="tpu_custom_call" | custom-call | flops 1 | bytes 1 | tf_op jit(solution)/shard_map/row_terms/pallas_call | solution.py:188
  46.7 2.5 %collective-permute-done.7.refs_1_.refs_7_ = bf16[2,128,2048]{2,1,0:T(8,128)(2,1)S(1)} collective-permute-done((bf16[2,128,2048]{2,1,0:T(8,128)(2,1)S(1)}, bf16[2,128,2048]{2,1,0:T(8,128)(2,1)S(1)}, u32[]{:S(2)}, u32[]{:S(2)}) %collective-permute-start.7) | collective-permute-done | bytes 1048608 | tf_op jit(solution)/shard_map/ppermute | solution.py:41
  49.2 4.3 %hidden_units.5 = (bf16[256,1024]{1,0:T(8,128)(2,1)S(1)}, bf16[256,1024]{1,0:T(8,128)(2,1)S(1)}, bf16[256,2048]{1,0:T(8,128)(2,1)S(1)}) custom-call(bf16[2,128,2048]{2,1,0:T(8,128)(2,1)S(1)} %collective-permute-done.6.refs_0_.refs_6_, bf16[2,128,2048]{2,1,0:T(8,128)(2,1)S(1)} %collective-permute-done.7.refs_1_.refs_7_, ...), custom_call_target="tpu_custom_call" | custom-call | flops 1 | bytes 1 | tf_op jit(solution)/shard_map/hidden_units/pallas_call | solution.py:121
  53.5 3.3 %row_terms.5 = (bf16[3,2,128,2048]{3,2,1,0:T(8,128)(2,1)S(1)}, bf16[3,2,128,2048]{3,2,1,0:T(8,128)(2,1)S(1)}) custom-call(bf16[256,1024]{1,0:T(8,128)(2,1)S(1)} %get-tuple-element.170.hidden_ref.refs_2_, bf16[256,1024]{1,0:T(8,128)(2,1)S(1)} %get-tuple-element.166.dpre_ref.refs_10_, ...), custom_call_target="tpu_custom_call", output_to_operand_aliasing={{0}: (4, {}), {1}: (5, {})} | custom-call | flops 1 | bytes 1 | tf_op jit(solution)/shard_map/row_terms/pallas_call | solution.py:188
  57.1 4.8 %weight_blocks.4 = (bf16[2,256,1024]{2,1,0:T(8,128)(2,1)S(1)}, bf16[2,256,1024]{2,1,0:T(8,128)(2,1)S(1)}) custom-call(s32[2]{0:T(128)S(1)} %copy-done.1, bf16[2,128,2048]{2,1,0:T(8,128)(2,1)S(1)} %copy-done, bf16[2,128,2048]{2,1,0:T(8,128)(2,1)S(1)} %collective-permute-done.refs_1_, bf16[2,128,2048]{2,1,0:T(8,128)(2,1)S(1)} %collective-permute-done.1.refs_0_.refs_2_, ...), custom_call_target="tpu_custom_call" | custom-call | flops 1 | bytes 1 | tf_op jit(solution)/shard_map/weight_blocks/pallas_call | solution.py:289
  65.2 4.4 %weight_blocks.5 = (bf16[2,512,512]{2,1,0:T(8,128)(2,1)S(1)}, bf16[2,512,512]{2,1,0:T(8,128)(2,1)S(1)}) custom-call(s32[2]{0:T(128)S(1)} %copy-done.1, bf16[256,1024]{1,0:T(8,128)(2,1)S(1)} %get-tuple-element.168.hidden_ref.refs_0_, bf16[512,1024]{1,0:T(8,128)(2,1)S(1)} %get-tuple-element.169.hidden_ref.refs_1_, ...), custom_call_target="tpu_custom_call" | custom-call | flops 1 | bytes 1 | tf_op jit(solution)/shard_map/weight_blocks/pallas_call | solution.py:289
  73.1 4.6 %weight_blocks.6.later_ref = bf16[4,256,1024]{2,1,0:T(8,128)(2,1)S(1)} custom-call(s32[2]{0:T(128)S(1)} %copy-done.1, bf16[2,128,2048]{2,1,0:T(8,128)(2,1)S(1)} %copy-done, bf16[2,128,2048]{2,1,0:T(8,128)(2,1)S(1)} %collective-permute-done.refs_1_, bf16[2,128,2048]{2,1,0:T(8,128)(2,1)S(1)} %collective-permute-done.1.refs_0_.refs_2_, ...), custom_call_target="tpu_custom_call" | custom-call | flops 1 | bytes 1 | tf_op jit(solution)/shard_map/weight_blocks/pallas_call | solution.py:289
  78.9 2.4 %collective-permute-start.10 = (bf16[2,2,128,2048]{3,2,1,0:T(8,128)(2,1)S(1)}, bf16[2,2,128,2048]{3,2,1,0:T(8,128)(2,1)S(1)}, u32[]{:S(2)}, u32[]{:S(2)}) collective-permute-start(bf16[2,2,128,2048]{3,2,1,0:T(8,128)(2,1)S(1)} %add_convert_fusion), channel_id=1, source_target_pairs={{0,6},{1,3},{2,0},{3,5},{4,2},{5,7},{6,4},{7,1},{8,14},{9,11},{10,... | collective-permute-start | bytes 6291464 | tf_op jit(solution)/shard_map/ppermute | solution.py:37
  81.2 4.3 %weight_blocks.7.later_ref = bf16[4,512,512]{2,1,0:T(8,128)(2,1)S(1)} custom-call(s32[2]{0:T(128)S(1)} %copy-done.1, bf16[256,1024]{1,0:T(8,128)(2,1)S(1)} %get-tuple-element.168.hidden_ref.refs_0_, bf16[512,1024]{1,0:T(8,128)(2,1)S(1)} %get-tuple-element.169.hidden_ref.refs_1_, bf16[256,1024]{1,0:T(8,128)(2,1)S(1)} %get-tuple-element.170.hidden_ref.refs_2_, ...), custom_call_target="tpu_custom_call" | custom-call | flops 1 | bytes 1 | tf_op jit(solution)/shard_map/weight_blocks/pallas_call | solution.py:289
  85.5 3.0 %collective-permute-done.11.b1 = bf16[2,256,1024]{2,1,0:T(8,128)(2,1)S(1)} collective-permute-done((bf16[2,256,1024]{2,1,0:T(8,128)(2,1)S(1)}, bf16[2,256,1024]{2,1,0:T(8,128)(2,1)S(1)}, u32[]{:S(2)}, u32[]{:S(2)}) %collective-permute-start.11) | collective-permute-done | bytes 1048608 | tf_op jit(solution)/shard_map/ppermute | solution.py:27
  90.5 6.4 %collective-permute-done.13.b1 = bf16[2,512,512]{2,1,0:T(8,128)(2,1)S(1)} collective-permute-done((bf16[2,512,512]{2,1,0:T(8,128)(2,1)S(1)}, bf16[2,512,512]{2,1,0:T(8,128)(2,1)S(1)}, u32[]{:S(2)}, u32[]{:S(2)}) %collective-permute-start.13) | collective-permute-done | bytes 1048608 | tf_op jit(solution)/shard_map/ppermute | solution.py:32
  98.7 2.4 %collective-permute-start.15 = (bf16[256,1024]{1,0:T(8,128)(2,1)S(1)}, bf16[256,1024]{1,0:T(8,128)(2,1)S(1)}, u32[]{:S(2)}, u32[]{:S(2)}) collective-permute-start(bf16[256,1024]{1,0:T(8,128)(2,1)S(1)} %get-tuple-element.210), channel_id=1, source_target_pairs={{0,32},{8,40},{16,48},{24,56},{32,64},{40,72},{48,80},{56,88},{64,... | collective-permute-start | bytes 1572872 | tf_op jit(solution)/shard_map/ppermute | solution.py:27
  101.4 3.0 %collective-permute-start.18 = (bf16[512,512]{1,0:T(8,128)(2,1)S(1)}, bf16[512,512]{1,0:T(8,128)(2,1)S(1)}, u32[]{:S(2)}, u32[]{:S(2)}) collective-permute-start(bf16[512,512]{1,0:T(8,128)(2,1)S(1)} %get-tuple-element.207), channel_id=1, source_target_pairs={{0,24},{8,0},{16,8},{24,16},{32,56},{40,32},{48,40},{56,48},{64,88... | collective-permute-start | bytes 1572872 | tf_op jit(solution)/shard_map/ppermute | solution.py:32
  104.4 8.6 %collective-permute-done.16.a1 = bf16[256,1024]{1,0:T(8,128)(2,1)S(1)} collective-permute-done((bf16[256,1024]{1,0:T(8,128)(2,1)S(1)}, bf16[256,1024]{1,0:T(8,128)(2,1)S(1)}, u32[]{:S(2)}, u32[]{:S(2)}) %collective-permute-start.16) | collective-permute-done | bytes 524320 | tf_op jit(solution)/shard_map/ppermute | solution.py:27
  112.9 2.3 %collective-permute-done.18.a1 = bf16[512,512]{1,0:T(8,128)(2,1)S(1)} collective-permute-done((bf16[512,512]{1,0:T(8,128)(2,1)S(1)}, bf16[512,512]{1,0:T(8,128)(2,1)S(1)}, u32[]{:S(2)}, u32[]{:S(2)}) %collective-permute-start.18) | collective-permute-done | bytes 524320 | tf_op jit(solution)/shard_map/ppermute | solution.py:32
  115.3 3.4 %collective-permute-done.17.b0 = bf16[512,512]{1,0:T(8,128)(2,1)S(1)} collective-permute-done((bf16[512,512]{1,0:T(8,128)(2,1)S(1)}, bf16[512,512]{1,0:T(8,128)(2,1)S(1)}, u32[]{:S(2)}, u32[]{:S(2)}) %collective-permute-start.17) | collective-permute-done | bytes 524320 | tf_op jit(solution)/shard_map/ppermute | solution.py:32
  134.0 3.4 %collective-permute-done.21 = bf16[128,1024]{1,0:T(8,128)(2,1)S(1)} collective-permute-done((bf16[128,1024]{1,0:T(8,128)(2,1)S(1)}, bf16[128,1024]{1,0:T(8,128)(2,1)S(1)}, u32[]{:S(2)}, u32[]{:S(2)}) %collective-permute-start.21) | collective-permute-done | bytes 262176 | tf_op jit(solution)/shard_map/ppermute | solution.py:32
  138.1 3.0 %collective-permute-done.25 = bf16[1024,128]{1,0:T(8,128)(2,1)S(1)} collective-permute-done((bf16[1024,128]{1,0:T(8,128)(2,1)S(1)}, bf16[1024,128]{1,0:T(8,128)(2,1)S(1)}, u32[]{:S(2)}, u32[]{:S(2)}) %collective-permute-start.25) | collective-permute-done | bytes 262176 | tf_op jit(solution)/shard_map/ppermute | solution.py:27
  (62 shorter events, 38.2 us)
Async XLA Ops:
  4.5 3.0 %collective-permute-start = (bf16[2,128,2048]{2,1,0:T(8,128)(2,1)}, bf16[2,128,2048]{2,1,0:T(8,128)(2,1)S(1)}, u32[]{:S(2)}, u32[]{:S(2)}) collective-permute-start(bf16[2,128,2048]{2,1,0:T(8,128)(2,1)} %get-tuple-element.156.refs_0_), channel_id=1, source_target_pairs={{0,1},{1,0},{2,3},{3,2},{4,5},{5,4},{6,7},{7,6},{8,9},{9,8},{10,11... | collective-permute-start | bytes 3145736 | tf_op jit(solution)/shard_map/ppermute | solution.py:41
  4.6 15.7 %collective-permute-start.1 = (bf16[2,128,2048]{2,1,0:T(8,128)(2,1)}, bf16[2,128,2048]{2,1,0:T(8,128)(2,1)S(1)}, u32[]{:S(2)}, u32[]{:S(2)}) collective-permute-start(bf16[2,128,2048]{2,1,0:T(8,128)(2,1)} %get-tuple-element.156.refs_0_), channel_id=1, source_target_pairs={{0,2},{1,7},{2,4},{3,1},{4,6},{5,3},{6,0},{7,5},{8,10},{9,15},{10,... | collective-permute-start | bytes 3145736 | tf_op jit(solution)/shard_map/ppermute | solution.py:37
  7.4 23.5 %collective-permute-start.2 = (bf16[2,128,2048]{2,1,0:T(8,128)(2,1)S(1)}, bf16[2,128,2048]{2,1,0:T(8,128)(2,1)S(1)}, u32[]{:S(2)}, u32[]{:S(2)}) collective-permute-start(bf16[2,128,2048]{2,1,0:T(8,128)(2,1)S(1)} %collective-permute-done.refs_1_), channel_id=1, source_target_pairs={{0,2},{1,7},{2,4},{3,1},{4,6},{5,3},{6,0},{7,5},{8,10},{9,15},{10,... | collective-permute-start | bytes 3145736 | tf_op jit(solution)/shard_map/ppermute | solution.py:37
  20.2 12.7 %collective-permute-start.3 = (bf16[2,128,2048]{2,1,0:T(8,128)(2,1)S(1)}, bf16[2,128,2048]{2,1,0:T(8,128)(2,1)S(1)}, u32[]{:S(2)}, u32[]{:S(2)}) collective-permute-start(bf16[2,128,2048]{2,1,0:T(8,128)(2,1)S(1)} %collective-permute-done.1.refs_0_.refs_2_), channel_id=1, source_target_pairs={{0,1},{1,0},{2,3},{3,2},{4,5},{5,4},{6,7},{7,6},{8,9},{9,8},{10,11... | collective-permute-start | bytes 3145736 | tf_op jit(solution)/shard_map/ppermute | solution.py:41
  20.3 12.7 %collective-permute-start.5 = (bf16[1,2,128,2048]{3,2,1,0:T(8,128)(2,1)S(1)}, bf16[1,2,128,2048]{3,2,1,0:T(8,128)(2,1)S(1)}, u32[]{:S(2)}, u32[]{:S(2)}) collective-permute-start(bf16[1,2,128,2048]{3,2,1,0:T(8,128)(2,1)S(1)} %get-tuple-element.116), channel_id=1, source_target_pairs={{0,1},{1,0},{2,3},{3,2},{4,5},{5,4},{6,7},{7,6},{8,9},{9,8},{10,11... | collective-permute-start | bytes 3145736 | tf_op jit(solution)/shard_map/ppermute | solution.py:41
  30.9 15.6 %collective-permute-start.6 = (bf16[2,128,2048]{2,1,0:T(8,128)(2,1)S(1)}, bf16[2,128,2048]{2,1,0:T(8,128)(2,1)S(1)}, u32[]{:S(2)}, u32[]{:S(2)}) collective-permute-start(bf16[2,128,2048]{2,1,0:T(8,128)(2,1)S(1)} %collective-permute-done.1.refs_0_.refs_2_), channel_id=1, source_target_pairs={{0,2},{1,7},{2,4},{3,1},{4,6},{5,3},{6,0},{7,5},{8,10},{9,15},{10,... | collective-permute-start | bytes 3145736 | tf_op jit(solution)/shard_map/ppermute | solution.py:37
  56.9 5.7 %collective-permute-start.8 = (bf16[3,2,128,2048]{3,2,1,0:T(8,128)(2,1)S(1)}, bf16[3,2,128,2048]{3,2,1,0:T(8,128)(2,1)S(1)}, u32[]{:S(2)}, u32[]{:S(2)}) collective-permute-start(bf16[3,2,128,2048]{3,2,1,0:T(8,128)(2,1)S(1)} %get-tuple-element.130), channel_id=1, source_target_pairs={{0,1},{1,0},{2,3},{3,2},{4,5},{5,4},{6,7},{7,6},{8,9},{9,8},{10,11... | collective-permute-start | bytes 9437192 | tf_op jit(solution)/shard_map/ppermute | solution.py:41
  63.0 14.9 %collective-permute-start.9 = (bf16[2,128,2048]{2,1,0:T(8,128)(2,1)S(1)}, bf16[2,128,2048]{2,1,0:T(8,128)(2,1)S(1)}, u32[]{:S(2)}, u32[]{:S(2)}) collective-permute-start(bf16[2,128,2048]{2,1,0:T(8,128)(2,1)S(1)} %fusion.3), channel_id=1, source_target_pairs={{0,6},{1,3},{2,0},{3,5},{4,2},{5,7},{6,4},{7,1},{8,14},{9,11},{10,... | collective-permute-start | bytes 3145736 | tf_op jit(solution)/shard_map/ppermute | solution.py:37
  63.2 25.3 %collective-permute-start.11 = (bf16[2,256,1024]{2,1,0:T(8,128)(2,1)S(1)}, bf16[2,256,1024]{2,1,0:T(8,128)(2,1)S(1)}, u32[]{:S(2)}, u32[]{:S(2)}) collective-permute-start(bf16[2,256,1024]{2,1,0:T(8,128)(2,1)S(1)} %get-tuple-element.143), channel_id=1, source_target_pairs={{0,32},{8,40},{16,48},{24,56},{32,64},{40,72},{48,80},{56,88},{64,... | collective-permute-start | bytes 3145736 | tf_op jit(solution)/shard_map/ppermute | solution.py:27
  63.6 26.8 %collective-permute-start.12 = (bf16[2,256,1024]{2,1,0:T(8,128)(2,1)S(1)}, bf16[2,256,1024]{2,1,0:T(8,128)(2,1)S(1)}, u32[]{:S(2)}, u32[]{:S(2)}) collective-permute-start(bf16[2,256,1024]{2,1,0:T(8,128)(2,1)S(1)} %get-tuple-element.144), channel_id=1, source_target_pairs={{0,96},{8,104},{16,112},{24,120},{32,0},{40,8},{48,16},{56,24},{64... | collective-permute-start | bytes 3145736 | tf_op jit(solution)/shard_map/ppermute | solution.py:27
  69.6 27.2 %collective-permute-start.13 = (bf16[2,512,512]{2,1,0:T(8,128)(2,1)S(1)}, bf16[2,512,512]{2,1,0:T(8,128)(2,1)S(1)}, u32[]{:S(2)}, u32[]{:S(2)}) collective-permute-start(bf16[2,512,512]{2,1,0:T(8,128)(2,1)S(1)} %get-tuple-element.154), channel_id=1, source_target_pairs={{0,8},{8,16},{16,24},{24,0},{32,40},{40,48},{48,56},{56,32},{64,72... | collective-permute-start | bytes 3145736 | tf_op jit(solution)/shard_map/ppermute | solution.py:32
  71.4 26.0 %collective-permute-start.14 = (bf16[2,512,512]{2,1,0:T(8,128)(2,1)S(1)}, bf16[2,512,512]{2,1,0:T(8,128)(2,1)S(1)}, u32[]{:S(2)}, u32[]{:S(2)}) collective-permute-start(bf16[2,512,512]{2,1,0:T(8,128)(2,1)S(1)} %get-tuple-element.155), channel_id=1, source_target_pairs={{0,24},{8,0},{16,8},{24,16},{32,56},{40,32},{48,40},{56,48},{64,88... | collective-permute-start | bytes 3145736 | tf_op jit(solution)/shard_map/ppermute | solution.py:32
  78.9 39.8 %collective-permute-start.10 = (bf16[2,2,128,2048]{3,2,1,0:T(8,128)(2,1)S(1)}, bf16[2,2,128,2048]{3,2,1,0:T(8,128)(2,1)S(1)}, u32[]{:S(2)}, u32[]{:S(2)}) collective-permute-start(bf16[2,2,128,2048]{3,2,1,0:T(8,128)(2,1)S(1)} %add_convert_fusion), channel_id=1, source_target_pairs={{0,6},{1,3},{2,0},{3,5},{4,2},{5,7},{6,4},{7,1},{8,14},{9,11},{10,... | collective-permute-start | bytes 6291464 | tf_op jit(solution)/shard_map/ppermute | solution.py:37
  97.8 15.1 %collective-permute-start.16 = (bf16[256,1024]{1,0:T(8,128)(2,1)S(1)}, bf16[256,1024]{1,0:T(8,128)(2,1)S(1)}, u32[]{:S(2)}, u32[]{:S(2)}) collective-permute-start(bf16[256,1024]{1,0:T(8,128)(2,1)S(1)} %get-tuple-element.209), channel_id=1, source_target_pairs={{0,96},{8,104},{16,112},{24,120},{32,0},{40,8},{48,16},{56,24},{64... | collective-permute-start | bytes 1572872 | tf_op jit(solution)/shard_map/ppermute | solution.py:27
  98.7 14.2 %collective-permute-start.15 = (bf16[256,1024]{1,0:T(8,128)(2,1)S(1)}, bf16[256,1024]{1,0:T(8,128)(2,1)S(1)}, u32[]{:S(2)}, u32[]{:S(2)}) collective-permute-start(bf16[256,1024]{1,0:T(8,128)(2,1)S(1)} %get-tuple-element.210), channel_id=1, source_target_pairs={{0,32},{8,40},{16,48},{24,56},{32,64},{40,72},{48,80},{56,88},{64,... | collective-permute-start | bytes 1572872 | tf_op jit(solution)/shard_map/ppermute | solution.py:27
  101.4 13.9 %collective-permute-start.18 = (bf16[512,512]{1,0:T(8,128)(2,1)S(1)}, bf16[512,512]{1,0:T(8,128)(2,1)S(1)}, u32[]{:S(2)}, u32[]{:S(2)}) collective-permute-start(bf16[512,512]{1,0:T(8,128)(2,1)S(1)} %get-tuple-element.207), channel_id=1, source_target_pairs={{0,24},{8,0},{16,8},{24,16},{32,56},{40,32},{48,40},{56,48},{64,88... | collective-permute-start | bytes 1572872 | tf_op jit(solution)/shard_map/ppermute | solution.py:32
  104.4 14.3 %collective-permute-start.17 = (bf16[512,512]{1,0:T(8,128)(2,1)S(1)}, bf16[512,512]{1,0:T(8,128)(2,1)S(1)}, u32[]{:S(2)}, u32[]{:S(2)}) collective-permute-start(bf16[512,512]{1,0:T(8,128)(2,1)S(1)} %get-tuple-element.208), channel_id=1, source_target_pairs={{0,8},{8,16},{16,24},{24,0},{32,40},{40,48},{48,56},{56,32},{64,72... | collective-permute-start | bytes 1572872 | tf_op jit(solution)/shard_map/ppermute | solution.py:32
  118.8 2.9 %collective-permute-start.19 = (bf16[2,128,2048]{2,1,0:T(8,128)(2,1)S(1)}, bf16[2,128,2048]{2,1,0:T(8,128)(2,1)S(1)}, u32[]{:S(2)}, u32[]{:S(2)}) collective-permute-start(bf16[2,128,2048]{2,1,0:T(8,128)(2,1)S(1)} %slice_bitcast_fusion), channel_id=1, source_target_pairs={{0,1},{1,0},{2,3},{3,2},{4,5},{5,4},{6,7},{7,6},{8,9},{9,8},{10,11... | collective-permute-start | bytes 3145736 | tf_op jit(solution)/shard_map/ppermute | solution.py:41
  121.7 10.7 %collective-permute-start.20 = (bf16[128,1024]{1,0:T(8,128)(2,1)S(1)}, bf16[128,1024]{1,0:T(8,128)(2,1)S(1)}, u32[]{:S(2)}, u32[]{:S(2)}) collective-permute-start(bf16[128,1024]{1,0:T(8,128)(2,1)S(1)} %get-tuple-element.192), channel_id=1, source_target_pairs={{0,16},{8,24},{16,0},{24,8},{32,48},{40,56},{48,32},{56,40},{64,80... | collective-permute-start | bytes 786440 | tf_op jit(solution)/shard_map/ppermute | solution.py:32
  121.8 15.6 %collective-permute-start.21 = (bf16[128,1024]{1,0:T(8,128)(2,1)S(1)}, bf16[128,1024]{1,0:T(8,128)(2,1)S(1)}, u32[]{:S(2)}, u32[]{:S(2)}) collective-permute-start(bf16[128,1024]{1,0:T(8,128)(2,1)S(1)} %get-tuple-element.193), channel_id=1, source_target_pairs={{0,8},{8,16},{16,24},{24,0},{32,40},{40,48},{48,56},{56,32},{64,72... | collective-permute-start | bytes 786440 | tf_op jit(solution)/shard_map/ppermute | solution.py:32
  122.9 14.5 %collective-permute-start.22 = (bf16[128,1024]{1,0:T(8,128)(2,1)S(1)}, bf16[128,1024]{1,0:T(8,128)(2,1)S(1)}, u32[]{:S(2)}, u32[]{:S(2)}) collective-permute-start(bf16[128,1024]{1,0:T(8,128)(2,1)S(1)} %get-tuple-element.194), channel_id=1, source_target_pairs={{0,24},{8,0},{16,8},{24,16},{32,56},{40,32},{48,40},{56,48},{64,88... | collective-permute-start | bytes 786440 | tf_op jit(solution)/shard_map/ppermute | solution.py:32
  125.1 12.3 %collective-permute-start.23 = (bf16[1024,128]{1,0:T(8,128)(2,1)S(1)}, bf16[1024,128]{1,0:T(8,128)(2,1)S(1)}, u32[]{:S(2)}, u32[]{:S(2)}) collective-permute-start(bf16[1024,128]{1,0:T(8,128)(2,1)S(1)} %get-tuple-element.196), channel_id=1, source_target_pairs={{0,64},{8,72},{16,80},{24,88},{32,96},{40,104},{48,112},{56,120},{... | collective-permute-start | bytes 786440 | tf_op jit(solution)/shard_map/ppermute | solution.py:27
  125.3 12.9 %collective-permute-start.24 = (bf16[1024,128]{1,0:T(8,128)(2,1)S(1)}, bf16[1024,128]{1,0:T(8,128)(2,1)S(1)}, u32[]{:S(2)}, u32[]{:S(2)}) collective-permute-start(bf16[1024,128]{1,0:T(8,128)(2,1)S(1)} %get-tuple-element.197), channel_id=1, source_target_pairs={{0,32},{8,40},{16,48},{24,56},{32,64},{40,72},{48,80},{56,88},{64,... | collective-permute-start | bytes 786440 | tf_op jit(solution)/shard_map/ppermute | solution.py:27
  132.4 8.7 %collective-permute-start.25 = (bf16[1024,128]{1,0:T(8,128)(2,1)S(1)}, bf16[1024,128]{1,0:T(8,128)(2,1)S(1)}, u32[]{:S(2)}, u32[]{:S(2)}) collective-permute-start(bf16[1024,128]{1,0:T(8,128)(2,1)S(1)} %get-tuple-element.198), channel_id=1, source_target_pairs={{0,96},{8,104},{16,112},{24,120},{32,0},{40,8},{48,16},{56,24},{64... | collective-permute-start | bytes 786440 | tf_op jit(solution)/shard_map/ppermute | solution.py:27
  (7 other events, 26.4 us)

commit v2 on v1

--- a/solution.py
+++ b/solution.py
@@ -95,8 +95,13 @@
 
 
 def hidden_units(packs, w_in, w_out):
+    halves = [(i, h) for i, p in enumerate(packs) for h in range(len(p))]
+    at = {p: k for k, p in enumerate(halves)}
+    where_r = [at[(i, 0)] for i in range(len(packs))]
+    where_d = [at[(i, len(p) - 1)] for i, p in enumerate(packs)]
+    flat = [a for p in packs for a in p]
     n = len(packs)
-    _, piece, width = packs[0].shape
+    _, piece, width = flat[0].shape
     count = n * piece
     hid = w_in.shape[1]
     tile = hid // SIDE
@@ -104,9 +109,10 @@
     strip = quarter // SIDE
 
     def body(*refs):
-        r = jnp.concatenate([ref[0] for ref in refs[:n]], axis=0)
-        d = jnp.concatenate([ref[1] for ref in refs[:n]], axis=0)
-        win_ref, wout_ref, hidden_ref, dpre_ref, turned_ref = refs[n:]
+        last = [refs[k].shape[0] - 1 for k in where_d]
+        r = jnp.concatenate([refs[k][0] for k in where_r], axis=0)
+        d = jnp.concatenate([refs[k][i] for k, i in zip(where_d, last)], axis=0)
+        win_ref, wout_ref, hidden_ref, dpre_ref, turned_ref = refs[len(flat) :]
         pre = dot(r, win_ref[...], ((1,), (0,)))
         dhid = dot(d, wout_ref[...], ((1,), (1,)))
         value, slope = gelu_parts(pre)
@@ -116,12 +122,14 @@
         for x in range(SIDE):
             at = pl.multiple_of(x * quarter + y * strip, strip)
             for k in range(n):
-                turned_ref[pl.ds(k * piece, piece), pl.ds(x * strip, strip)] = refs[k][1, :, pl.ds(at, strip)]
+                turned_ref[pl.ds(k * piece, piece), pl.ds(x * strip, strip)] = refs[where_d[k]][
+                    last[k], :, pl.ds(at, strip)
+                ]
 
     return pl.pallas_call(
         body,
         grid=(SIDE,),
-        in_specs=[whole(a) for a in packs]
+        in_specs=[whole(a) for a in flat]
         + [
             pl.BlockSpec((width, tile), lambda j: (0, j)),
             pl.BlockSpec((tile, width), lambda j: (j, 0)),
@@ -139,7 +147,7 @@
         compiler_params=params(4 + count // 64),
         cost_estimate=LITTLE,
         name="hidden_units",
-    )(*packs, held(w_in), held(w_out))
+    )(*flat, held(w_in), held(w_out))
 
 
 def hold(w_in, w_out):
@@ -169,7 +177,7 @@
     return pltpu.with_memory_space_constraint(w, pltpu.VMEM)
 
 
-def row_terms(hidden, dpre, w_in, w_out, piece, groups, held_terms=()):
+def row_terms(hidden, dpre, w_in, w_out, piece, groups, first=0, held_terms=()):
     count, hid = hidden.shape
     width = w_in.shape[0]
     n = count // (2 * piece)
@@ -184,7 +192,6 @@
                 for s, v in enumerate((ffn, dx)):
                     outs[h][k, s] = v[(h * n + k) * piece : (h * n + k + 1) * piece]
 
-    first = groups - 1 if held_terms else 0
     return pl.pallas_call(
         body,
         grid=(SIDE,),
@@ -353,39 +360,44 @@
     w_in, w_out = hold(*after((w_in, w_out), own_mine))
     near_mine = move_lane(own_mine, 1)
     own_other = swap_core(own_mine)
-    own_packs = [own_mine, own_other]
-    own = hidden_units(own_packs, w_in, w_out)
+    own = hidden_units([[own_mine], [own_other]], w_in, w_out)
 
     near_other = move_lane(own_other, 1)
+    near_mine = after(near_mine, own)
+    far_mine = move_lane(near_mine, 1)
+    swapped_mine = [swap_core(near_mine[:1]), swap_core(near_mine[1:])]
     own_terms = row_terms(own[0], own[1], w_in, w_out, routed, 1)
     own_got = swap_core(own_terms[1])
-    near_mine = after(near_mine, own)
-    far_mine = move_lane(near_mine, 1)
-    near_packs = [near_mine, near_other, swap_core(near_mine), swap_core(near_other)]
-    near_packs, own_got = after((near_packs, own_got), own)
-    near = hidden_units(near_packs, w_in, w_out)
-
+    near_mine, swapped_mine = after((near_mine, swapped_mine), own_terms)
+    near = hidden_units([[near_mine], swapped_mine], w_in, w_out)
     near_terms = row_terms(near[0], near[1], w_in, w_out, routed, 3)
-    far_mine = after(far_mine, near_terms)
-    far_packs = [far_mine, swap_core(far_mine)]
-    far = hidden_units(far_packs, w_in, w_out)
-    last_terms = row_terms(far[0], far[1], w_in, w_out, routed, 3, near_terms)
+
+    near_other = after(near_other, near)
+    swapped_other = [swap_core(near_other[:1]), swap_core(near_other[1:])]
+    swapped_other, own_got = after((swapped_other, own_got), near_terms)
+    other = hidden_units([[near_other], swapped_other], w_in, w_out)
+    near_terms = row_terms(other[0], other[1], w_in, w_out, routed, 3, 1, near_terms)
+
+    far_mine = after(far_mine, other)
+    far_packs = after([far_mine, swap_core(far_mine)], near_terms)
+    far = hidden_units([[p] for p in far_packs], w_in, w_out)
+    last_terms = row_terms(far[0], far[1], w_in, w_out, routed, 3, 2, near_terms)
     last_got = swap_core(last_terms[1])
 
-    all_packs = own_packs + near_packs + far_packs
-    hidden, dpre, turned = ([u[i] for u in (own, near, far)] for i in range(3))
+    all_packs = [own_mine, own_other, near_mine, swapped_mine[0], near_other, swapped_other[0]] + far_packs
+    hidden, dpre, turned = ([u[i] for u in (own, near, other, far)] for i in range(3))
     all_packs, dpre = after((all_packs, dpre), last_terms)
     in_up, in_down = in_blocks(me, all_packs, dpre, first_step, True)
     in_below, in_above = move_x(in_up, 1), move_x(in_down, -1)
 
-    last_got = after(last_got, in_up, in_down)
+    hidden, turned = after((hidden, turned), in_up, in_down)
+    out_up, out_down = out_blocks(me, hidden, turned, first_step, True)
+    out_below, out_above = move_y(out_up, 1), move_y(out_down, -1)
+
+    last_got = after(last_got, out_up, out_down)
     to_far = (last_terms[0][2].astype(F32) + last_got[2].astype(F32)).astype(BF16)
     z_far = move_lane(to_far, -1)
-
-    hidden, turned = after((hidden, turned), to_far)
-    out_up, out_down = out_blocks(me, hidden, turned, first_step, True)
-    out_below, out_above = move_y(out_up, 1), move_y(out_down, -1)
-    all_packs, dpre = after((all_packs, dpre), out_up, out_down)
+    all_packs, dpre = after((all_packs, dpre), to_far)
     in_later = in_blocks(me, all_packs, dpre, later_step, False)[0]
     z_far = after(z_far, in_later)
     passed = jnp.pad(z_far.astype(F32)[None], ((0, 1), (0, 0), (0, 0), (0, 0)))

time: 143 us -> 139 us (0.972)
  waiting for transfers between devices: 50.8 us -> 45.5 us
  Pallas kernels: 55.7 us -> 58 us
  starting transfers between devices: 26.6 us -> 25.1 us
    ppermute x7, waiting for transfers between devices: 18.2 us -> 13.6 us  [move_y(): return lax.ppermute(v, 'ctx', perm)]
    ppermute x7 -> x9, waiting for transfers between devices: 5.01 us -> 1.2 us  [swap_core(): return lax.ppermute(v, 'head', [(i, i ^ 1) for i in range(2 * SIDE)])]
    ppermute x5, starting transfers between devices: 7.92 us -> 5.6 us  [move_lane(): return lax.ppermute(v, 'head', perm)]
    ppermute x7, waiting for transfers between devices: 17.3 us -> 19.4 us  [move_x(): return lax.ppermute(v, 'ctx', perm)]
    pallas_call x3 -> x4, Pallas kernels: 15.9 us -> 17.2 us  [hidden_units(): pl.pallas_call(body, grid=(SIDE,), in_specs=[whole(a) for a in flat] + [p...]
    pallas_call x3 -> x4, Pallas kernels: 12.3 us -> 13.2 us  [row_terms(): pl.pallas_call(body, grid=(SIDE,), in_specs=[whole(hidden), whole(dpre),...]
  transfers between devices with their start and end apart: 26 -> 28, of which waited for: 17 -> 16; matrix products, arithmetic and copies ran while one was open for 4% -> 5% of each run, Pallas kernels for 31% -> 34%
where the time goes in v2:
time: 139 us
  Pallas kernels  58 us (42%)
  waiting for transfers between devices  45.5 us (33%)
  starting transfers between devices  25.1 us (18%)
  other arithmetic  6.14 us (4%)
  matrix products  2.14 us (2%)
  between operations  1.62 us (1%)
    ppermute x7, waiting for transfers between devices, move_x(): return lax.ppermute(v, 'ctx', perm)  19.4 us
    pallas_call x4, Pallas kernels, blocks_call(): pl.pallas_call(body, grid_spec=pltpu.PrefetchScalarGridSpec(num_scalar_pr...  18.1 us
    pallas_call x4, Pallas kernels, hidden_units(): pl.pallas_call(body, grid=(SIDE,), in_specs=[whole(a) for a in flat] + [p...  17.2 us
    ppermute x7, waiting for transfers between devices, move_y(): return lax.ppermute(v, 'ctx', perm)  13.6 us
    pallas_call x4, Pallas kernels, row_terms(): pl.pallas_call(body, grid=(SIDE,), in_specs=[whole(hidden), whole(dpre),...  13.2 us
    ppermute x5, waiting for transfers between devices, move_lane(): return lax.ppermute(v, 'head', perm)  11.3 us
    ppermute x7, starting transfers between devices, move_y(): return lax.ppermute(v, 'ctx', perm)  9.64 us
    ppermute x7, starting transfers between devices, move_x(): return lax.ppermute(v, 'ctx', perm)  7.61 us
  transfers between devices with their start and end apart: 28, of which 16 were waited for; matrix products, arithmetic and copies ran while one was open for 5% of the time, Pallas kernels for 34%

profile of v2, /device:TPU:70, one launch (start us, length us, event | category | flops | bytes accessed | tf_op | source)
XLA Modules:
  0.0 138.8 jit_solution(11268107738988349783)
XLA Ops:
  1.3 3.2 %take_rows.1 = (bf16[2,128,2048]{2,1,0:T(8,128)(2,1)}, s32[2]{0:T(128)}) custom-call(s32[1]{0:T(128)S(6)} %copy.20.counts_ref, bf16[512,2048]{1,0:T(8,128)(2,1)} %tokens_ref.1, s32[1,128]{1,0:T(1,128)} %bitcast.31, f32[1,128]{1,0:T(1,128)} %bitcast.30, bf16[128,2048]{1,0:T(8,128)(2,1)} %cotan_ref.1), custom_call_target="tpu_custom_call" | custom-call | flops 1 | bytes 1 | tf_op jit(solution)/shard_map/take_rows/pallas_call | solution.py:74
  9.0 3.5 %hold_weights.1 = (bf16[2048,1024]{1,0:T(8,128)(2,1)S(1)}, bf16[1024,2048]{1,0:T(8,128)(2,1)S(1)}) custom-call(bf16[2048,1024]{1,0:T(8,128)(2,1)} %win_ref, bf16[1024,2048]{1,0:T(8,128)(2,1)} %wout_ref), custom_call_target="tpu_custom_call" | custom-call | flops 1 | bytes 1 | tf_op jit(solution)/shard_map/hold_weights/pallas_call | solution.py:164
  12.5 4.3 %hidden_units.4 = (bf16[256,1024]{1,0:T(8,128)(2,1)S(1)}, bf16[256,1024]{1,0:T(8,128)(2,1)S(1)}, bf16[256,2048]{1,0:T(8,128)(2,1)S(1)}) custom-call(bf16[2,128,2048]{2,1,0:T(8,128)(2,1)S(1)} %copy-done, bf16[2,128,2048]{2,1,0:T(8,128)(2,1)S(1)} %collective-permute-done.refs_1_, bf16[2048,1024]{1,0:T(8,128)(2,1)S(1)} %get-tuple-element.124.refs_2_.win_ref.refs_3_, ...), custom_call_target="tpu_custom_call" | custom-call | flops 1 | bytes 1 | tf_op jit(solution)/shard_map/hidden_units/pallas_call | solution.py:129
  16.9 2.8 %collective-permute-done.2.refs_0_.refs_2_ = bf16[2,128,2048]{2,1,0:T(8,128)(2,1)S(1)} collective-permute-done((bf16[2,128,2048]{2,1,0:T(8,128)(2,1)}, bf16[2,128,2048]{2,1,0:T(8,128)(2,1)S(1)}, u32[]{:S(2)}, u32[]{:S(2)}) %collective-permute-start.2) | collective-permute-done | bytes 1048608 | tf_op jit(solution)/shard_map/ppermute | solution.py:37
  20.3 3.3 %row_terms.4 = (bf16[1,2,128,2048]{3,2,1,0:T(8,128)(2,1)S(1)}, bf16[1,2,128,2048]{3,2,1,0:T(8,128)(2,1)S(1)}) custom-call(bf16[256,1024]{1,0:T(8,128)(2,1)S(1)} %get-tuple-element.196.hidden_ref.refs_0_, bf16[256,1024]{1,0:T(8,128)(2,1)S(1)} %get-tuple-element.191.dpre_ref.refs_8_, bf16[2048,1024]{1,0:T(8,128)(2,1)S(1)} %get-tuple-element.124.refs_2_.win_ref.refs_3_, ...), custom_call_target="tpu_custom_call" | custom-call | flops 1 | bytes 1 | tf_op jit(solution)/shard_map/row_terms/pallas_call | solution.py:195
  25.8 4.3 %hidden_units.5 = (bf16[256,1024]{1,0:T(8,128)(2,1)S(1)}, bf16[256,1024]{1,0:T(8,128)(2,1)S(1)}, bf16[256,2048]{1,0:T(8,128)(2,1)S(1)}) custom-call(bf16[2,128,2048]{2,1,0:T(8,128)(2,1)S(1)} %collective-permute-done.2.refs_0_.refs_2_, bf16[1,128,2048]{2,1,0:T(8,128)(2,1)S(1)} %collective-permute-done.3.refs_1_.refs_3_, ...), custom_call_target="tpu_custom_call" | custom-call | flops 1 | bytes 1 | tf_op jit(solution)/shard_map/hidden_units/pallas_call | solution.py:129
  31.6 3.3 %row_terms.5 = (bf16[3,2,128,2048]{3,2,1,0:T(8,128)(2,1)S(1)}, bf16[3,2,128,2048]{3,2,1,0:T(8,128)(2,1)S(1)}) custom-call(bf16[256,1024]{1,0:T(8,128)(2,1)S(1)} %get-tuple-element.197.hidden_ref.refs_1_, bf16[256,1024]{1,0:T(8,128)(2,1)S(1)} %get-tuple-element.192.dpre_ref.refs_9_, bf16[2048,1024]{1,0:T(8,128)(2,1)S(1)} %get-tuple-element.124.refs_2_.win_ref.refs_3_, ...), custom_call_target="tpu_custom_call" | custom-call | flops 1 | bytes 1 | tf_op jit(solution)/shard_map/row_terms/pallas_call | solution.py:195
  34.9 4.3 %hidden_units.6 = (bf16[256,1024]{1,0:T(8,128)(2,1)S(1)}, bf16[256,1024]{1,0:T(8,128)(2,1)S(1)}, bf16[256,2048]{1,0:T(8,128)(2,1)S(1)}) custom-call(bf16[2,128,2048]{2,1,0:T(8,128)(2,1)S(1)} %collective-permute-done.1.refs_0_.refs_4_, bf16[1,128,2048]{2,1,0:T(8,128)(2,1)S(1)} %collective-permute-done.5.refs_1_.refs_5_, ...), custom_call_target="tpu_custom_call" | custom-call | flops 1 | bytes 1 | tf_op jit(solution)/shard_map/hidden_units/pallas_call | solution.py:129
  39.2 2.9 %collective-permute-done.8.refs_0_.refs_6_ = bf16[2,128,2048]{2,1,0:T(8,128)(2,1)S(1)} collective-permute-done((bf16[2,128,2048]{2,1,0:T(8,128)(2,1)S(1)}, bf16[2,128,2048]{2,1,0:T(8,128)(2,1)S(1)}, u32[]{:S(2)}, u32[]{:S(2)}) %collective-permute-start.8) | collective-permute-done | bytes 1048608 | tf_op jit(solution)/shard_map/ppermute | solution.py:37
  42.1 3.3 %row_terms.6 = (bf16[3,2,128,2048]{3,2,1,0:T(8,128)(2,1)S(1)}, bf16[3,2,128,2048]{3,2,1,0:T(8,128)(2,1)S(1)}) custom-call(bf16[256,1024]{1,0:T(8,128)(2,1)S(1)} %get-tuple-element.198.hidden_ref.refs_2_, bf16[256,1024]{1,0:T(8,128)(2,1)S(1)} %get-tuple-element.193.dpre_ref.refs_10_, ...), custom_call_target="tpu_custom_call", output_to_operand_aliasing={{0}: (4, {}), {1}: (5, {})} | custom-call | flops 1 | bytes 1 | tf_op jit(solution)/shard_map/row_terms/pallas_call | solution.py:195
  45.4 4.3 %hidden_units.7 = (bf16[256,1024]{1,0:T(8,128)(2,1)S(1)}, bf16[256,1024]{1,0:T(8,128)(2,1)S(1)}, bf16[256,2048]{1,0:T(8,128)(2,1)S(1)}) custom-call(bf16[2,128,2048]{2,1,0:T(8,128)(2,1)S(1)} %collective-permute-done.8.refs_0_.refs_6_, bf16[2,128,2048]{2,1,0:T(8,128)(2,1)S(1)} %collective-permute-done.9.refs_1_.refs_7_, ...), custom_call_target="tpu_custom_call" | custom-call | flops 1 | bytes 1 | tf_op jit(solution)/shard_map/hidden_units/pallas_call | solution.py:129
  49.8 3.3 %row_terms.7 = (bf16[3,2,128,2048]{3,2,1,0:T(8,128)(2,1)S(1)}, bf16[3,2,128,2048]{3,2,1,0:T(8,128)(2,1)S(1)}) custom-call(bf16[256,1024]{1,0:T(8,128)(2,1)S(1)} %get-tuple-element.199.hidden_ref.refs_3_, bf16[256,1024]{1,0:T(8,128)(2,1)S(1)} %get-tuple-element.194.dpre_ref.refs_11_, ...), custom_call_target="tpu_custom_call", output_to_operand_aliasing={{0}: (4, {}), {1}: (5, {})} | custom-call | flops 1 | bytes 1 | tf_op jit(solution)/shard_map/row_terms/pallas_call | solution.py:195
  53.9 4.7 %weight_blocks.4 = (bf16[2,256,1024]{2,1,0:T(8,128)(2,1)S(1)}, bf16[2,256,1024]{2,1,0:T(8,128)(2,1)S(1)}) custom-call(s32[2]{0:T(128)S(1)} %copy-done.1, bf16[2,128,2048]{2,1,0:T(8,128)(2,1)S(1)} %copy-done, bf16[2,128,2048]{2,1,0:T(8,128)(2,1)S(1)} %collective-permute-done.refs_1_, bf16[2,128,2048]{2,1,0:T(8,128)(2,1)S(1)} %collective-permute-done.2.refs_0_.refs_2_, ...), custom_call_target="tpu_custom_call" | custom-call | flops 1 | bytes 1 | tf_op jit(solution)/shard_map/weight_blocks/pallas_call | solution.py:296
  58.6 4.5 %weight_blocks.5 = (bf16[2,512,512]{2,1,0:T(8,128)(2,1)S(1)}, bf16[2,512,512]{2,1,0:T(8,128)(2,1)S(1)}) custom-call(s32[2]{0:T(128)S(1)} %copy-done.1, bf16[256,1024]{1,0:T(8,128)(2,1)S(1)} %get-tuple-element.196.hidden_ref.refs_0_, bf16[256,1024]{1,0:T(8,128)(2,1)S(1)} %get-tuple-element.197.hidden_ref.refs_1_, ...), custom_call_target="tpu_custom_call" | custom-call | flops 1 | bytes 1 | tf_op jit(solution)/shard_map/weight_blocks/pallas_call | solution.py:296
  69.0 4.5 %weight_blocks.6.later_ref = bf16[4,256,1024]{2,1,0:T(8,128)(2,1)S(1)} custom-call(s32[2]{0:T(128)S(1)} %copy-done.1, bf16[2,128,2048]{2,1,0:T(8,128)(2,1)S(1)} %copy-done, bf16[2,128,2048]{2,1,0:T(8,128)(2,1)S(1)} %collective-permute-done.refs_1_, bf16[2,128,2048]{2,1,0:T(8,128)(2,1)S(1)} %collective-permute-done.2.refs_0_.refs_2_, ...), custom_call_target="tpu_custom_call" | custom-call | flops 1 | bytes 1 | tf_op jit(solution)/shard_map/weight_blocks/pallas_call | solution.py:296
  73.5 4.9 %collective-permute-done.11 = bf16[2,128,2048]{2,1,0:T(8,128)(2,1)S(1)} collective-permute-done((bf16[2,128,2048]{2,1,0:T(8,128)(2,1)S(1)}, bf16[2,128,2048]{2,1,0:T(8,128)(2,1)S(1)}, u32[]{:S(2)}, u32[]{:S(2)}) %collective-permute-start.11) | collective-permute-done | bytes 1048608 | tf_op jit(solution)/shard_map/ppermute | solution.py:37
  79.6 4.4 %weight_blocks.7.later_ref = bf16[4,512,512]{2,1,0:T(8,128)(2,1)S(1)} custom-call(s32[2]{0:T(128)S(1)} %copy-done.1, bf16[256,1024]{1,0:T(8,128)(2,1)S(1)} %get-tuple-element.196.hidden_ref.refs_0_, bf16[256,1024]{1,0:T(8,128)(2,1)S(1)} %get-tuple-element.197.hidden_ref.refs_1_, bf16[256,1024]{1,0:T(8,128)(2,1)S(1)} %get-tuple-element.198.hidden_ref.refs_2_, ...), custom_call_target="tpu_custom_call" | custom-call | flops 1 | bytes 1 | tf_op jit(solution)/shard_map/weight_blocks/pallas_call | solution.py:296
  83.9 5.0 %collective-permute-done.13.b1 = bf16[2,256,1024]{2,1,0:T(8,128)(2,1)S(1)} collective-permute-done((bf16[2,256,1024]{2,1,0:T(8,128)(2,1)S(1)}, bf16[2,256,1024]{2,1,0:T(8,128)(2,1)S(1)}, u32[]{:S(2)}, u32[]{:S(2)}) %collective-permute-start.13) | collective-permute-done | bytes 1048608 | tf_op jit(solution)/shard_map/ppermute | solution.py:27
  94.5 2.4 %collective-permute-start.17 = (bf16[256,1024]{1,0:T(8,128)(2,1)S(1)}, bf16[256,1024]{1,0:T(8,128)(2,1)S(1)}, u32[]{:S(2)}, u32[]{:S(2)}) collective-permute-start(bf16[256,1024]{1,0:T(8,128)(2,1)S(1)} %get-tuple-element.240), channel_id=1, source_target_pairs={{0,32},{8,40},{16,48},{24,56},{32,64},{40,72},{48,80},{56,88},{64,... | collective-permute-start | bytes 1572872 | tf_op jit(solution)/shard_map/ppermute | solution.py:27
  97.2 3.0 %collective-permute-start.20 = (bf16[512,512]{1,0:T(8,128)(2,1)S(1)}, bf16[512,512]{1,0:T(8,128)(2,1)S(1)}, u32[]{:S(2)}, u32[]{:S(2)}) collective-permute-start(bf16[512,512]{1,0:T(8,128)(2,1)S(1)} %get-tuple-element.237), channel_id=1, source_target_pairs={{0,24},{8,0},{16,8},{24,16},{32,56},{40,32},{48,40},{56,48},{64,88... | collective-permute-start | bytes 1572872 | tf_op jit(solution)/shard_map/ppermute | solution.py:32
  100.2 8.5 %collective-permute-done.18.a1 = bf16[256,1024]{1,0:T(8,128)(2,1)S(1)} collective-permute-done((bf16[256,1024]{1,0:T(8,128)(2,1)S(1)}, bf16[256,1024]{1,0:T(8,128)(2,1)S(1)}, u32[]{:S(2)}, u32[]{:S(2)}) %collective-permute-start.18) | collective-permute-done | bytes 524320 | tf_op jit(solution)/shard_map/ppermute | solution.py:27
  111.1 3.4 %collective-permute-done.19.b0 = bf16[512,512]{1,0:T(8,128)(2,1)S(1)} collective-permute-done((bf16[512,512]{1,0:T(8,128)(2,1)S(1)}, bf16[512,512]{1,0:T(8,128)(2,1)S(1)}, u32[]{:S(2)}, u32[]{:S(2)}) %collective-permute-start.19) | collective-permute-done | bytes 524320 | tf_op jit(solution)/shard_map/ppermute | solution.py:32
  129.8 3.4 %collective-permute-done.23 = bf16[128,1024]{1,0:T(8,128)(2,1)S(1)} collective-permute-done((bf16[128,1024]{1,0:T(8,128)(2,1)S(1)}, bf16[128,1024]{1,0:T(8,128)(2,1)S(1)}, u32[]{:S(2)}, u32[]{:S(2)}) %collective-permute-start.23) | collective-permute-done | bytes 262176 | tf_op jit(solution)/shard_map/ppermute | solution.py:32
  134.0 3.0 %collective-permute-done.27 = bf16[1024,128]{1,0:T(8,128)(2,1)S(1)} collective-permute-done((bf16[1024,128]{1,0:T(8,128)(2,1)S(1)}, bf16[1024,128]{1,0:T(8,128)(2,1)S(1)}, u32[]{:S(2)}, u32[]{:S(2)}) %collective-permute-start.27) | collective-permute-done | bytes 262176 | tf_op jit(solution)/shard_map/ppermute | solution.py:27
  (70 shorter events, 42.6 us)
Async XLA Ops:
  4.6 15.1 %collective-permute-start.2 = (bf16[2,128,2048]{2,1,0:T(8,128)(2,1)}, bf16[2,128,2048]{2,1,0:T(8,128)(2,1)S(1)}, u32[]{:S(2)}, u32[]{:S(2)}) collective-permute-start(bf16[2,128,2048]{2,1,0:T(8,128)(2,1)} %get-tuple-element.183.refs_0_), channel_id=1, source_target_pairs={{0,2},{1,7},{2,4},{3,1},{4,6},{5,3},{6,0},{7,5},{8,10},{9,15},{10,... | collective-permute-start | bytes 3145736 | tf_op jit(solution)/shard_map/ppermute | solution.py:37
  7.4 23.5 %collective-permute-start.1 = (bf16[2,128,2048]{2,1,0:T(8,128)(2,1)S(1)}, bf16[2,128,2048]{2,1,0:T(8,128)(2,1)S(1)}, u32[]{:S(2)}, u32[]{:S(2)}) collective-permute-start(bf16[2,128,2048]{2,1,0:T(8,128)(2,1)S(1)} %collective-permute-done.refs_1_), channel_id=1, source_target_pairs={{0,2},{1,7},{2,4},{3,1},{4,6},{5,3},{6,0},{7,5},{8,10},{9,15},{10,... | collective-permute-start | bytes 3145736 | tf_op jit(solution)/shard_map/ppermute | solution.py:37
  19.8 6.1 %collective-permute-start.4 = (bf16[1,128,2048]{2,1,0:T(8,128)(2,1)S(1)}, bf16[1,128,2048]{2,1,0:T(8,128)(2,1)S(1)}, u32[]{:S(2)}, u32[]{:S(2)}) collective-permute-start(bf16[1,128,2048]{2,1,0:T(8,128)(2,1)S(1)} %get-tuple-element.245), channel_id=1, source_target_pairs={{0,1},{1,0},{2,3},{3,2},{4,5},{5,4},{6,7},{7,6},{8,9},{9,8},{10,11... | collective-permute-start | bytes 1572872 | tf_op jit(solution)/shard_map/ppermute | solution.py:41
  19.9 6.0 %collective-permute-start.3 = (bf16[1,128,2048]{2,1,0:T(8,128)(2,1)S(1)}, bf16[1,128,2048]{2,1,0:T(8,128)(2,1)S(1)}, u32[]{:S(2)}, u32[]{:S(2)}) collective-permute-start(bf16[1,128,2048]{2,1,0:T(8,128)(2,1)S(1)} %get-tuple-element.246), channel_id=1, source_target_pairs={{0,1},{1,0},{2,3},{3,2},{4,5},{5,4},{6,7},{7,6},{8,9},{9,8},{10,11... | collective-permute-start | bytes 1572872 | tf_op jit(solution)/shard_map/ppermute | solution.py:41
  23.7 11.2 %collective-permute-start.7 = (bf16[1,2,128,2048]{3,2,1,0:T(8,128)(2,1)S(1)}, bf16[1,2,128,2048]{3,2,1,0:T(8,128)(2,1)S(1)}, u32[]{:S(2)}, u32[]{:S(2)}) collective-permute-start(bf16[1,2,128,2048]{3,2,1,0:T(8,128)(2,1)S(1)} %get-tuple-element.131), channel_id=1, source_target_pairs={{0,1},{1,0},{2,3},{3,2},{4,5},{5,4},{6,7},{7,6},{8,9},{9,8},{10,11... | collective-permute-start | bytes 3145736 | tf_op jit(solution)/shard_map/ppermute | solution.py:41
  23.8 18.3 %collective-permute-start.8 = (bf16[2,128,2048]{2,1,0:T(8,128)(2,1)S(1)}, bf16[2,128,2048]{2,1,0:T(8,128)(2,1)S(1)}, u32[]{:S(2)}, u32[]{:S(2)}) collective-permute-start(bf16[2,128,2048]{2,1,0:T(8,128)(2,1)S(1)} %collective-permute-done.2.refs_0_.refs_2_), channel_id=1, source_target_pairs={{0,2},{1,7},{2,4},{3,1},{4,6},{5,3},{6,0},{7,5},{8,10},{9,15},{10,... | collective-permute-start | bytes 3145736 | tf_op jit(solution)/shard_map/ppermute | solution.py:37
  31.0 3.9 %collective-permute-start.6 = (bf16[1,128,2048]{2,1,0:T(8,128)(2,1)S(1)}, bf16[1,128,2048]{2,1,0:T(8,128)(2,1)S(1)}, u32[]{:S(2)}, u32[]{:S(2)}) collective-permute-start(bf16[1,128,2048]{2,1,0:T(8,128)(2,1)S(1)} %get-tuple-element.243), channel_id=1, source_target_pairs={{0,1},{1,0},{2,3},{3,2},{4,5},{5,4},{6,7},{7,6},{8,9},{9,8},{10,11... | collective-permute-start | bytes 1572872 | tf_op jit(solution)/shard_map/ppermute | solution.py:41
  53.1 10.0 %collective-permute-start.10 = (bf16[3,2,128,2048]{3,2,1,0:T(8,128)(2,1)S(1)}, bf16[3,2,128,2048]{3,2,1,0:T(8,128)(2,1)S(1)}, u32[]{:S(2)}, u32[]{:S(2)}) collective-permute-start(bf16[3,2,128,2048]{3,2,1,0:T(8,128)(2,1)S(1)} %get-tuple-element.155), channel_id=1, source_target_pairs={{0,1},{1,0},{2,3},{3,2},{4,5},{5,4},{6,7},{7,6},{8,9},{9,8},{10,11... | collective-permute-start | bytes 9437192 | tf_op jit(solution)/shard_map/ppermute | solution.py:41
  63.5 14.9 %collective-permute-start.11 = (bf16[2,128,2048]{2,1,0:T(8,128)(2,1)S(1)}, bf16[2,128,2048]{2,1,0:T(8,128)(2,1)S(1)}, u32[]{:S(2)}, u32[]{:S(2)}) collective-permute-start(bf16[2,128,2048]{2,1,0:T(8,128)(2,1)S(1)} %fusion.3), channel_id=1, source_target_pairs={{0,6},{1,3},{2,0},{3,5},{4,2},{5,7},{6,4},{7,1},{8,14},{9,11},{10,... | collective-permute-start | bytes 3145736 | tf_op jit(solution)/shard_map/ppermute | solution.py:37
  63.7 25.3 %collective-permute-start.13 = (bf16[2,256,1024]{2,1,0:T(8,128)(2,1)S(1)}, bf16[2,256,1024]{2,1,0:T(8,128)(2,1)S(1)}, u32[]{:S(2)}, u32[]{:S(2)}) collective-permute-start(bf16[2,256,1024]{2,1,0:T(8,128)(2,1)S(1)} %get-tuple-element.170), channel_id=1, source_target_pairs={{0,32},{8,40},{16,48},{24,56},{32,64},{40,72},{48,80},{56,88},{64,... | collective-permute-start | bytes 3145736 | tf_op jit(solution)/shard_map/ppermute | solution.py:27
  64.2 26.8 %collective-permute-start.14 = (bf16[2,256,1024]{2,1,0:T(8,128)(2,1)S(1)}, bf16[2,256,1024]{2,1,0:T(8,128)(2,1)S(1)}, u32[]{:S(2)}, u32[]{:S(2)}) collective-permute-start(bf16[2,256,1024]{2,1,0:T(8,128)(2,1)S(1)} %get-tuple-element.171), channel_id=1, source_target_pairs={{0,96},{8,104},{16,112},{24,120},{32,0},{40,8},{48,16},{56,24},{64... | collective-permute-start | bytes 3145736 | tf_op jit(solution)/shard_map/ppermute | solution.py:27
  65.7 27.0 %collective-permute-start.15 = (bf16[2,512,512]{2,1,0:T(8,128)(2,1)S(1)}, bf16[2,512,512]{2,1,0:T(8,128)(2,1)S(1)}, u32[]{:S(2)}, u32[]{:S(2)}) collective-permute-start(bf16[2,512,512]{2,1,0:T(8,128)(2,1)S(1)} %get-tuple-element.180), channel_id=1, source_target_pairs={{0,8},{8,16},{16,24},{24,0},{32,40},{40,48},{48,56},{56,32},{64,72... | collective-permute-start | bytes 3145736 | tf_op jit(solution)/shard_map/ppermute | solution.py:32
  67.3 25.9 %collective-permute-start.16 = (bf16[2,512,512]{2,1,0:T(8,128)(2,1)S(1)}, bf16[2,512,512]{2,1,0:T(8,128)(2,1)S(1)}, u32[]{:S(2)}, u32[]{:S(2)}) collective-permute-start(bf16[2,512,512]{2,1,0:T(8,128)(2,1)S(1)} %get-tuple-element.181), channel_id=1, source_target_pairs={{0,24},{8,0},{16,8},{24,16},{32,56},{40,32},{48,40},{56,48},{64,88... | collective-permute-start | bytes 3145736 | tf_op jit(solution)/shard_map/ppermute | solution.py:32
  79.4 35.1 %collective-permute-start.12 = (bf16[2,2,128,2048]{3,2,1,0:T(8,128)(2,1)S(1)}, bf16[2,2,128,2048]{3,2,1,0:T(8,128)(2,1)S(1)}, u32[]{:S(2)}, u32[]{:S(2)}) collective-permute-start(bf16[2,2,128,2048]{3,2,1,0:T(8,128)(2,1)S(1)} %add_convert_fusion), channel_id=1, source_target_pairs={{0,6},{1,3},{2,0},{3,5},{4,2},{5,7},{6,4},{7,1},{8,14},{9,11},{10,... | collective-permute-start | bytes 6291464 | tf_op jit(solution)/shard_map/ppermute | solution.py:37
  93.6 15.1 %collective-permute-start.18 = (bf16[256,1024]{1,0:T(8,128)(2,1)S(1)}, bf16[256,1024]{1,0:T(8,128)(2,1)S(1)}, u32[]{:S(2)}, u32[]{:S(2)}) collective-permute-start(bf16[256,1024]{1,0:T(8,128)(2,1)S(1)} %get-tuple-element.239), channel_id=1, source_target_pairs={{0,96},{8,104},{16,112},{24,120},{32,0},{40,8},{48,16},{56,24},{64... | collective-permute-start | bytes 1572872 | tf_op jit(solution)/shard_map/ppermute | solution.py:27
  94.5 14.2 %collective-permute-start.17 = (bf16[256,1024]{1,0:T(8,128)(2,1)S(1)}, bf16[256,1024]{1,0:T(8,128)(2,1)S(1)}, u32[]{:S(2)}, u32[]{:S(2)}) collective-permute-start(bf16[256,1024]{1,0:T(8,128)(2,1)S(1)} %get-tuple-element.240), channel_id=1, source_target_pairs={{0,32},{8,40},{16,48},{24,56},{32,64},{40,72},{48,80},{56,88},{64,... | collective-permute-start | bytes 1572872 | tf_op jit(solution)/shard_map/ppermute | solution.py:27
  97.2 13.9 %collective-permute-start.20 = (bf16[512,512]{1,0:T(8,128)(2,1)S(1)}, bf16[512,512]{1,0:T(8,128)(2,1)S(1)}, u32[]{:S(2)}, u32[]{:S(2)}) collective-permute-start(bf16[512,512]{1,0:T(8,128)(2,1)S(1)} %get-tuple-element.237), channel_id=1, source_target_pairs={{0,24},{8,0},{16,8},{24,16},{32,56},{40,32},{48,40},{56,48},{64,88... | collective-permute-start | bytes 1572872 | tf_op jit(solution)/shard_map/ppermute | solution.py:32
  100.2 14.3 %collective-permute-start.19 = (bf16[512,512]{1,0:T(8,128)(2,1)S(1)}, bf16[512,512]{1,0:T(8,128)(2,1)S(1)}, u32[]{:S(2)}, u32[]{:S(2)}) collective-permute-start(bf16[512,512]{1,0:T(8,128)(2,1)S(1)} %get-tuple-element.238), channel_id=1, source_target_pairs={{0,8},{8,16},{16,24},{24,0},{32,40},{40,48},{48,56},{56,32},{64,72... | collective-permute-start | bytes 1572872 | tf_op jit(solution)/shard_map/ppermute | solution.py:32
  117.6 10.7 %collective-permute-start.22 = (bf16[128,1024]{1,0:T(8,128)(2,1)S(1)}, bf16[128,1024]{1,0:T(8,128)(2,1)S(1)}, u32[]{:S(2)}, u32[]{:S(2)}) collective-permute-start(bf16[128,1024]{1,0:T(8,128)(2,1)S(1)} %get-tuple-element.222), channel_id=1, source_target_pairs={{0,16},{8,24},{16,0},{24,8},{32,48},{40,56},{48,32},{56,40},{64,80... | collective-permute-start | bytes 786440 | tf_op jit(solution)/shard_map/ppermute | solution.py:32
  117.6 15.6 %collective-permute-start.23 = (bf16[128,1024]{1,0:T(8,128)(2,1)S(1)}, bf16[128,1024]{1,0:T(8,128)(2,1)S(1)}, u32[]{:S(2)}, u32[]{:S(2)}) collective-permute-start(bf16[128,1024]{1,0:T(8,128)(2,1)S(1)} %get-tuple-element.223), channel_id=1, source_target_pairs={{0,8},{8,16},{16,24},{24,0},{32,40},{40,48},{48,56},{56,32},{64,72... | collective-permute-start | bytes 786440 | tf_op jit(solution)/shard_map/ppermute | solution.py:32
  118.8 14.5 %collective-permute-start.24 = (bf16[128,1024]{1,0:T(8,128)(2,1)S(1)}, bf16[128,1024]{1,0:T(8,128)(2,1)S(1)}, u32[]{:S(2)}, u32[]{:S(2)}) collective-permute-start(bf16[128,1024]{1,0:T(8,128)(2,1)S(1)} %get-tuple-element.224), channel_id=1, source_target_pairs={{0,24},{8,0},{16,8},{24,16},{32,56},{40,32},{48,40},{56,48},{64,88... | collective-permute-start | bytes 786440 | tf_op jit(solution)/shard_map/ppermute | solution.py:32
  121.0 12.3 %collective-permute-start.25 = (bf16[1024,128]{1,0:T(8,128)(2,1)S(1)}, bf16[1024,128]{1,0:T(8,128)(2,1)S(1)}, u32[]{:S(2)}, u32[]{:S(2)}) collective-permute-start(bf16[1024,128]{1,0:T(8,128)(2,1)S(1)} %get-tuple-element.226), channel_id=1, source_target_pairs={{0,64},{8,72},{16,80},{24,88},{32,96},{40,104},{48,112},{56,120},{... | collective-permute-start | bytes 786440 | tf_op jit(solution)/shard_map/ppermute | solution.py:27
  121.1 12.9 %collective-permute-start.26 = (bf16[1024,128]{1,0:T(8,128)(2,1)S(1)}, bf16[1024,128]{1,0:T(8,128)(2,1)S(1)}, u32[]{:S(2)}, u32[]{:S(2)}) collective-permute-start(bf16[1024,128]{1,0:T(8,128)(2,1)S(1)} %get-tuple-element.227), channel_id=1, source_target_pairs={{0,32},{8,40},{16,48},{24,56},{32,64},{40,72},{48,80},{56,88},{64,... | collective-permute-start | bytes 786440 | tf_op jit(solution)/shard_map/ppermute | solution.py:27
  128.3 8.7 %collective-permute-start.27 = (bf16[1024,128]{1,0:T(8,128)(2,1)S(1)}, bf16[1024,128]{1,0:T(8,128)(2,1)S(1)}, u32[]{:S(2)}, u32[]{:S(2)}) collective-permute-start(bf16[1024,128]{1,0:T(8,128)(2,1)S(1)} %get-tuple-element.228), channel_id=1, source_target_pairs={{0,96},{8,104},{16,112},{24,120},{32,0},{40,8},{48,16},{56,24},{64... | collective-permute-start | bytes 786440 | tf_op jit(solution)/shard_map/ppermute | solution.py:27
  (9 other events, 40.2 us)
